TPU v7x, 1024 devices: a whole 8x8x8 slice. The times are simulated.
1024 devices in a mesh: expert: 64 (over y, z), dp: 16 (over x, core).
Axes of the slice: x: 8, y: 8, z: 8, core: 2. Of those that a mesh axis runs over, the one named last changes fastest.
Arguments:
- tokens: bfloat16 [8192, 1664], P('expert', 'dp'), may hold values from -6 to 6
- cotangent: bfloat16 [8192, 1664], P('expert', 'dp'), may hold values from -6 to 6
- routes: int32 [8192, 2], P('expert'), may hold values from 0 to 63, all different within a row; in each aligned block of 128 rows (0 to 127, 128 to 255, ...) at most 8 rows name the same one
- router: bfloat16 [1664, 64], replicated, may hold values from -3 to 3
- w_in: bfloat16 [64, 1664, 8192], P('expert', None, 'dp'), may hold values from -0.15625 to 0.15625
- w_out: bfloat16 [64, 8192, 1664], P('expert', 'dp'), may hold values from -0.0625 to 0.0625
Outputs:
- mixed: bfloat16 [8192, 1664], P('expert', 'dp')
- token_grad: bfloat16 [8192, 1664], P('expert', 'dp')
- router_grad: float32 [1664, 64], P('dp')
Inputs may be any that keep to these rules, and one draw needn't show every extreme that they name: Each token names two different experts. Among the 256 routes of one index of expert, no expert is named more than 8 times, a bound that some block reaches.
All inputs are finite; a program needn't handle non-finite values.
Results may differ from a plain program's by a relative error of at most 0.035.
Values may be sent and summed in bfloat16 or wider, within the bound.
No kernel may reach another device: no remote copies, remote signals or barrier semaphores. Data moves between devices by JAX's collectives and lax.ppermute only.
A program may use at most 32 MiB of HBM per device.

v0:
```python
import jax
import jax.numpy as jnp
from jax import lax
from jax.sharding import PartitionSpec as P


def folded(shard, axis, dim, absorb, carry):
    whole = jax.tree.map(lambda part: lax.all_gather(part, axis, axis=dim, tiled=True), shard)
    return absorb(carry, whole, jnp.int32(0))


def gelu_grad(preact, upstream):
    return jax.vjp(jax.nn.gelu, preact)[1](upstream)[0]


def shards(tokens, cotangent, routes, router, w_in, w_out):
    tok_count, feat_width = tokens.shape
    experts = router.shape[1]
    sources = lax.axis_size("expert")
    capacity = max(2, 4 * tok_count // experts)
    slot_total = sources * capacity
    flat_routes = routes.reshape(-1)
    one_hot = (flat_routes[:, None] == jnp.arange(experts, dtype=jnp.int32)[None, :]).astype(
        jnp.int32
    )
    slot_rank = jnp.sum(jnp.cumsum(one_hot, axis=0) * one_hot, axis=1) - 1
    target = flat_routes * capacity + slot_rank

    def place(values):
        empty = jnp.zeros((experts * capacity, feat_width), values.dtype)
        return (
            empty.at[target]
            .set(jnp.repeat(values, 2, axis=0))
            .reshape(experts, capacity, feat_width)
        )

    got_tokens, got_cot = (
        lax.all_to_all(place(tokens), "expert", split_axis=0, concat_axis=0, tiled=True),
        lax.all_to_all(place(cotangent), "expert", split_axis=0, concat_axis=0, tiled=True),
    )
    slot_tokens = got_tokens.reshape(slot_total, feat_width)
    slot_cot = got_cot.reshape(slot_total, feat_width)
    first_w = w_in[0]
    second_w = w_out[0]
    hidden_width = first_w.shape[1]

    def fold_tokens(running, feature_piece, offset):
        preact = jnp.dot(feature_piece, first_w, preferred_element_type=jnp.float32)
        scores = jnp.dot(feature_piece, router, preferred_element_type=jnp.float32)
        return (preact, scores)

    def fold_cotangent(running, feature_piece, offset):
        return lax.dot_general(
            feature_piece, second_w, (((1,), (1,)), ((), ())), preferred_element_type=jnp.float32
        )

    start_tokens = (
        jnp.zeros((slot_total, hidden_width), jnp.float32),
        jnp.zeros((slot_total, experts), jnp.float32),
    )
    start_cot = jnp.zeros((slot_total, hidden_width), jnp.float32)
    folders = (fold_tokens, fold_cotangent)
    starts = (start_tokens, start_cot)
    members = (slot_tokens, slot_cot)
    results = []
    for member_index in range(2):
        results.append(
            folded(members[member_index], "dp", 1, folders[member_index], starts[member_index])
        )
    preact, scores = results[0]
    grad_proj = results[1]
    expert_id = lax.axis_index("expert")
    own_expert = (jnp.arange(experts, dtype=jnp.int32) == expert_id).astype(jnp.float32)
    chances = jax.nn.softmax(scores, axis=-1)
    gating = jnp.sum(chances * own_expert[None, :], axis=1)
    hidden = jax.nn.gelu(preact).astype(jnp.bfloat16)
    out_term = gating[:, None] * jnp.dot(hidden, second_w, preferred_element_type=jnp.float32)
    gate_term = jnp.sum(hidden.astype(jnp.float32) * grad_proj, axis=1)
    pre_grad = gelu_grad(preact, gating[:, None] * grad_proj).astype(jnp.bfloat16)
    back_term = lax.dot_general(
        pre_grad, first_w, (((1,), (1,)), ((), ())), preferred_element_type=jnp.float32
    )
    groups = lax.axis_size("dp")
    spread = jnp.broadcast_to(gate_term[:, None], (slot_total, groups))
    out_sum, back_sum, gate_sum = (
        lax.psum_scatter(
            out_term.astype(jnp.bfloat16), "dp", scatter_dimension=1, tiled=True
        ).astype(jnp.float32),
        lax.psum_scatter(
            back_term.astype(jnp.bfloat16), "dp", scatter_dimension=1, tiled=True
        ).astype(jnp.float32),
        lax.psum_scatter(spread.astype(jnp.bfloat16), "dp", scatter_dimension=1, tiled=True).astype(
            jnp.float32
        ),
    )
    gate_grad = gate_sum[:, 0]
    score_grad = ((gate_grad * gating)[:, None] * (own_expert[None, :] - chances)).astype(
        jnp.bfloat16
    )
    router_slice = lax.dynamic_slice_in_dim(
        router, lax.axis_index("dp") * feat_width, feat_width, 0
    )
    router_back = lax.dot_general(
        score_grad, router_slice, (((1,), (1,)), ((), ())), preferred_element_type=jnp.float32
    )
    slot_grad = (back_sum + router_back).astype(jnp.bfloat16)
    router_part = lax.dot_general(
        slot_tokens, score_grad, (((0,), (0,)), ((), ())), preferred_element_type=jnp.float32
    )
    router_grad = lax.psum(router_part, "expert")
    slot_out = out_sum.astype(jnp.bfloat16).reshape(sources, capacity, feat_width)
    back_out, back_grad = (
        lax.all_to_all(slot_out, "expert", split_axis=0, concat_axis=0, tiled=True),
        lax.all_to_all(
            slot_grad.reshape(sources, capacity, feat_width),
            "expert",
            split_axis=0,
            concat_axis=0,
            tiled=True,
        ),
    )
    pair_out = (
        back_out.reshape(experts * capacity, feat_width)[target]
        .reshape(tok_count, 2, feat_width)
        .astype(jnp.float32)
    )
    pair_grad = (
        back_grad.reshape(experts * capacity, feat_width)[target]
        .reshape(tok_count, 2, feat_width)
        .astype(jnp.float32)
    )
    mixed = (pair_out[:, 0] + pair_out[:, 1]).astype(jnp.bfloat16)
    token_grad = (pair_grad[:, 0] + pair_grad[:, 1]).astype(jnp.bfloat16)
    return (mixed, token_grad, router_grad)


def solution(mesh):
    placed = (
        P("expert", "dp"),
        P("expert", "dp"),
        P("expert", None),
        P(),
        P("expert", None, "dp"),
        P("expert", "dp", None),
    )
    return jax.shard_map(
        shards,
        mesh=mesh,
        in_specs=placed,
        out_specs=(P("expert", "dp"), P("expert", "dp"), P("dp", None)),
        check_vma=False,
    )
```

profile of v0, /device:TPU:16, one launch (start us, length us, event | category | flops | bytes accessed | tf_op | source)
XLA Modules:
  0.0 523.1 jit_solution(8199005157718466143)
XLA Ops:
  7.2 1.0 copy.40
  8.2 0.1 eq.39
  8.3 0.1 eq.35
  8.5 0.7 broadcast_multiply_fusion
  9.2 0.6 reduce-window.6
  9.8 0.2 slice_reduce_fusion
  10.0 0.1 fusion.25
  10.1 0.1 copy.39
  10.2 0.1 mul.112
  10.4 0.8 copy.43
  11.3 1.2 scatter_custom_fusion
  12.5 34.7 %all_to_all.20 = bf16[64,8,104]{2,1,0:T(8,128)(2,1)S(1)} all-to-all(bf16[64,8,104]{2,1,0:T(8,128)(2,1)S(1)} %bitcast.64), channel_id=1, replica_groups=mesh['expert'=64,'dp'=16] {'expert'}, dimensions={0} | all-to-all | bytes 212992 | tf_op jit(solution)/shard_map/all_to_all | solution.py:38
  47.2 0.8 copy.44
  48.0 0.0 all-gather.5.cloned.1.call-start
  48.1 0.8 copy.48
  49.0 1.2 scatter_custom_fusion.1
  50.2 16.8 %all_to_all.21 = bf16[64,8,104]{2,1,0:T(8,128)(2,1)S(1)} all-to-all(bf16[64,8,104]{2,1,0:T(8,128)(2,1)S(1)} %bitcast.63), channel_id=1, replica_groups=mesh['expert'=64,'dp'=16] {'expert'}, dimensions={0} | all-to-all | bytes 212992 | tf_op jit(solution)/shard_map/all_to_all | solution.py:39
  66.9 0.7 copy.49
  67.8 16.8 %all-gather.3.cloned.1.call-done = bf16[512,1664]{0,1:T(8,128)(2,1)} async-done(((bf16[512,104]{0,1:T(8,128)(2,1)}), bf16[512,1664]{0,1:T(8,128)(2,1)}) %all-gather.3.cloned.1.call-update) | async-done | bytes 1703952 | tf_op jit(solution)/shard_map/all_gather | solution.py:8
  84.6 2.0 fusion.46
  86.7 0.1 multiply_reduce_fusion.1
  86.8 2.6 fusion.4
  89.4 41.8 %all-gather.5.cloned.1.call-done = bf16[512,1664]{0,1:T(8,128)(2,1)} async-done(((bf16[512,104]{0,1:T(8,128)(2,1)}), bf16[512,1664]{0,1:T(8,128)(2,1)}) %all-gather.5.cloned.1.call-update) | async-done | bytes 1703952 | tf_op jit(solution)/shard_map/all_gather | solution.py:8
  131.2 2.9 multiply_reduce_fusion
  134.1 2.6 convolution_convert_fusion
  136.8 2.4 multiply_convert_fusion
  139.2 1.3 dynamic-slice
  140.5 47.1 %all-reduce = bf16[512,16]{0,1:T(8,128)(2,1)S(1)} all-reduce(bf16[512,16]{0,1:T(8,128)(2,1)S(1)} %broadcast_in_dim.8), channel_id=4, replica_groups=mesh['expert'=64,'dp'=16] {'dp'}, use_global_device_ids=true, to_apply=%region_11.12.clone | all-reduce | flops 8192 | bytes 32768
  187.5 0.7 fusion.34
  188.2 0.1 multiply_convert_fusion.2
  188.3 11.7 %reduce-scatter.5.cloned.1.call-done = bf16[512,104]{0,1:T(8,128)(2,1)} async-done(((bf16[512,1664]{0,1:T(8,128)(2,1)}), bf16[512,104]{0,1:T(8,128)(2,1)}) %reduce-scatter.5.cloned.1.call-update) | async-done | bytes 106512 | tf_op jit(solution)/shard_map/reduce_scatter | solution.py:89
  200.0 1.2 fusion.6
  201.2 0.8 copy.50
  202.0 14.2 %all-to-all-start.3 = ((bf16[64,8,104]{2,1,0:T(8,128)(2,1)}), bf16[64,8,104]{2,1,0:T(8,128)(2,1)S(1)}, u32[]{:S(2)}, u32[]{:S(2)}) async-start(bf16[64,8,104]{2,1,0:T(8,128)(2,1)} %bitcast.18), calls=%async_computation.5 | async-start | bytes 262144 | tf_op jit(solution)/shard_map/all_to_all | solution.py:114
  216.1 0.2 fusion.36
  216.3 266.9 %psum.7 = f32[104,64]{0,1:T(8,128)} all-reduce(f32[104,64]{0,1:T(8,128)S(1)} %fusion.36), channel_id=1, replica_groups=mesh['expert'=64,'dp'=16] {'expert'}, use_global_device_ids=true, to_apply=%region_12.13 | all-reduce | flops 6656 | bytes 53248 | tf_op jit(solution)/shard_map/psum | solution.py:110
  483.2 1.6 copy.45
  484.9 18.1 %all-to-all-start.1 = ((bf16[64,8,104]{2,1,0:T(8,128)(2,1)}), bf16[64,8,104]{2,1,0:T(8,128)(2,1)S(1)}, u32[]{:S(2)}, u32[]{:S(2)}) async-start(bf16[64,8,104]{2,1,0:T(8,128)(2,1)} %bitcast.8), calls=%async_computation.2 | async-start | bytes 262144 | tf_op jit(solution)/shard_map/all_to_all | solution.py:113
  503.0 0.9 gather_fusion.1
  503.9 0.1 fusion.44
  504.0 0.1 copy.55
  504.1 0.1 copy.56
  504.2 10.6 %all-to-all-done.1 = bf16[64,8,104]{2,1,0:T(8,128)(2,1)S(1)} async-done(((bf16[64,8,104]{2,1,0:T(8,128)(2,1)}), bf16[64,8,104]{2,1,0:T(8,128)(2,1)S(1)}, u32[]{:S(2)}, u32[]{:S(2)}) %all-to-all-start.1) | async-done | bytes 106528 | tf_op jit(solution)/shard_map/all_to_all | solution.py:113
  514.8 0.9 gather_fusion
  515.6 0.1 fusion.45
  515.7 0.1 copy.53
  515.8 0.1 copy.54
  515.9 0.6 fusion.31
  (28 shorter events, 0.4 us)
Async XLA Ops:
  7.2 124.0 %copy-start = (bf16[1,512,1664]{2,1,0:T(8,128)(2,1)S(1)}, bf16[1,512,1664]{2,1,0:T(8,128)(2,1)}, u32[]{:S(2)}) copy-start(bf16[1,512,1664]{2,1,0:T(8,128)(2,1)} %param.11) | copy-start | bytes 5111812
  7.2 77.4 %copy-start.2 = (bf16[1664,64]{0,1:T(8,128)(2,1)S(1)}, bf16[1664,64]{0,1:T(8,128)(2,1)}, u32[]{:S(2)}) copy-start(bf16[1664,64]{0,1:T(8,128)(2,1)} %param.9) | copy-start | bytes 638980
  7.2 77.4 %all-gather.3.cloned.1.call-start = ((), (), s32[]{:S(2)}) async-start(), calls=%async_computation.6 | async-start | bytes 1810432 | tf_op jit(solution)/shard_map/all_gather | solution.py:8
  48.0 83.2 %all-gather.5.cloned.1.call-start = ((), (), s32[]{:S(2)}) async-start(), calls=%async_computation.8 | async-start | bytes 1810432 | tf_op jit(solution)/shard_map/all_gather | solution.py:8
  67.7 132.3 %reduce-scatter.5.cloned.1.call-start = ((), (), s32[]{:S(2)}) async-start(), calls=%async_computation.9 | async-start | bytes 1810432 | tf_op jit(solution)/shard_map/reduce_scatter | solution.py:89
  84.6 2.2 copy-start.1
  131.2 2.9 copy-start.3
  136.7 346.5 %reduce-scatter.3.cloned.1.call-start = ((), (), s32[]{:S(2)}) async-start(), calls=%async_computation.7 | async-start | bytes 1810432 | tf_op jit(solution)/shard_map/reduce_scatter | solution.py:86
  202.0 282.9 %all-to-all-start.3 = ((bf16[64,8,104]{2,1,0:T(8,128)(2,1)}), bf16[64,8,104]{2,1,0:T(8,128)(2,1)S(1)}, u32[]{:S(2)}, u32[]{:S(2)}) async-start(bf16[64,8,104]{2,1,0:T(8,128)(2,1)} %bitcast.18), calls=%async_computation.5 | async-start | bytes 262144 | tf_op jit(solution)/shard_map/all_to_all | solution.py:114
  484.9 29.9 %all-to-all-start.1 = ((bf16[64,8,104]{2,1,0:T(8,128)(2,1)}), bf16[64,8,104]{2,1,0:T(8,128)(2,1)S(1)}, u32[]{:S(2)}, u32[]{:S(2)}) async-start(bf16[64,8,104]{2,1,0:T(8,128)(2,1)} %bitcast.8), calls=%async_computation.2 | async-start | bytes 262144 | tf_op jit(solution)/shard_map/all_to_all | solution.py:113
Sparse Core Ops, SparseCore 0:
  48.1 36.4 all-gather.2
  87.3 43.8 all-gather.4
  136.8 63.1 reduce-scatter.4
  203.7 63.1 reduce-scatter.2
where the time goes:
time: 524 us; the launch traced here: 523 us
  blocking collectives  365 us (70%)
  waiting for transfers between devices  81 us (15%)
  starting transfers between devices  32.5 us (6%)
  between operations  14 us (3%)
  matrix products  13.8 us (3%)
  local copies, waits for them, and re-layouts  13.3 us (3%)
    psum x1, blocking collectives, shards(): router_grad = lax.psum(router_part, 'expert')  267 us
    all_gather x2, waiting for transfers between devices, folded(): lax.all_gather(part, axis, axis=dim, tiled=True)  58.6 us
    unnamed x1, blocking collectives  47.1 us
    all_to_all x1, blocking collectives, shards(): lax.all_to_all(place(tokens), 'expert', split_axis=0, concat_axis=0, tile...  34.7 us
    all_to_all x1, starting transfers between devices, shards(): lax.all_to_all(slot_out, 'expert', split_axis=0, concat_axis=0, tiled=True)  18.1 us
    all_to_all x1, blocking collectives, shards(): lax.all_to_all(place(cotangent), 'expert', split_axis=0, concat_axis=0, t...  16.8 us
    all_to_all x1, starting transfers between devices, shards(): lax.all_to_all(slot_grad.reshape(sources, capacity, feat_width), 'expert'...  14.2 us
    reduce_scatter x1, waiting for transfers between devices, shards(): lax.psum_scatter(back_term.astype(jnp.bfloat16), 'dp', scatter_dimension=...  11.7 us
  transfers between devices with their start and end apart: 6, of which 4 were waited for; matrix products, arithmetic and copies ran while one was open for 3% of the time, Pallas kernels for 0%

commit v1 on v0

v1 whole, which is shorter than its diff:
```python
import functools

import jax
import jax.numpy as jnp
import numpy as np
from jax import lax
from jax.experimental import pallas as pl
from jax.experimental.pallas import tpu as pltpu
from jax.sharding import PartitionSpec as P

F32 = jnp.float32
BF16 = jnp.bfloat16
VMEM_LIMIT = 48 * 1024 * 1024
VMEM = pl.BlockSpec(memory_space=pltpu.VMEM)
SMEM = pl.BlockSpec(memory_space=pltpu.SMEM)


def dot(a, b, dims=((1,), (0,))):
    return lax.dot_general(a, b, (dims, ((), ())), preferred_element_type=F32)


def call(body, out_shape, in_specs, flops=10_000_000, moved=1_000_000):
    return pl.pallas_call(
        body,
        out_shape=out_shape,
        in_specs=in_specs,
        out_specs=jax.tree.map(lambda _: VMEM, out_shape),
        compiler_params=pltpu.CompilerParams(vmem_limit_bytes=VMEM_LIMIT),
        cost_estimate=pl.CostEstimate(flops=flops, bytes_accessed=moved, transcendentals=0),
    )


def place_kernel(capacity, experts, routes_ref, tok_ref, cot_ref, slots_ref, pick_ref):
    rows, width = tok_ref.shape
    slots = slots_ref.shape[0]
    routes = routes_ref[...]
    lane = lax.broadcasted_iota(jnp.int32, (rows, experts), 1)
    hot = [(routes[:, k : k + 1] == lane).astype(F32) for k in range(2)]
    before = lax.broadcasted_iota(jnp.int32, (rows, rows), 0) > lax.broadcasted_iota(
        jnp.int32, (rows, rows), 1
    )
    before = before.astype(BF16)
    first = dot(before, hot[0].astype(BF16))
    second = dot(before, hot[1].astype(BF16)) + jnp.sum(hot[0], axis=0, keepdims=True)
    rank = [
        jnp.sum(first * hot[0], axis=1, keepdims=True),
        jnp.sum(second * hot[1], axis=1, keepdims=True),
    ]
    place = lax.broadcasted_iota(jnp.int32, (rows, slots), 1)
    target = [routes[:, k : k + 1] * capacity + rank[k].astype(jnp.int32) for k in range(2)]
    pick = ((place == target[0]) | (place == target[1])).astype(F32).astype(BF16)
    pick_ref[...] = pick
    slots_ref[:, :width] = dot(pick, tok_ref[...], ((0,), (0,))).astype(BF16)
    slots_ref[:, width:] = dot(pick, cot_ref[...], ((0,), (0,))).astype(BF16)


def expert_kernel(
    hidden_width,
    experts,
    at_ref,
    got_ref,
    w_ref,
    keep_ref,
    send_ref,
    gate_ref,
    chance_ref,
    acc,
    both,
    scale,
):
    phase, step = pl.program_id(0), pl.program_id(1)
    per_step = got_ref.shape[0]
    slots = got_ref.shape[1]
    width = got_ref.shape[2] // 2
    ff = hidden_width

    @pl.when(phase == 0)
    def _():
        total = dot(got_ref[0], w_ref[0])
        for j in range(1, per_step):
            total = total + dot(got_ref[j], w_ref[j])

        @pl.when(step == 0)
        def _():
            acc[...] = total

        @pl.when(step > 0)
        def _():
            acc[...] += total

    @pl.when((phase == 0) & (step == pl.num_programs(1) - 1))
    def _():
        chunk = 64
        own = at_ref[0]

        def one(i, carry):
            rows = pl.ds(pl.multiple_of(i * chunk, chunk), chunk)
            scores = acc[rows, 2 * ff :]
            lane = lax.broadcasted_iota(jnp.int32, scores.shape, 1)
            scores = jnp.where(lane < experts, scores, -jnp.inf)
            top = jnp.max(scores, axis=1, keepdims=True)
            raised = jnp.exp(scores - top)
            chances = raised / jnp.sum(raised, axis=1, keepdims=True)
            gating = jnp.sum(jnp.where(lane == own, chances, 0.0), axis=1, keepdims=True)
            x = acc[rows, :ff]
            proj = acc[rows, ff : 2 * ff]
            c = np.float32(np.sqrt(2.0 / np.pi))
            square = x * x
            t = jnp.tanh(c * (x + 0.044715 * (square * x)))
            half = 0.5 * (1.0 + t)
            hidden = (x * half).astype(BF16)
            slope = half + 0.5 * x * (1.0 - t * t) * (c * (1.0 + 3 * 0.044715 * square))
            both[rows, :ff] = (slope * (gating * proj)).astype(BF16)
            both[rows, ff:] = hidden
            gate = jnp.sum(hidden.astype(F32) * proj, axis=1, keepdims=True)
            acc[rows, 2 * ff :] = jnp.where(lane == experts, gate, chances)
            wide = lax.broadcasted_iota(jnp.int32, (chunk, 2 * width), 1)
            scale[rows, :] = jnp.where(wide < width, 1.0, gating)
            return carry

        lax.fori_loop(0, slots // chunk, one, 0)
        turned = acc[:, 2 * ff :].T
        chance_ref[...] = turned[:experts]
        gate_ref[...] = turned[experts : experts + 8]

    @pl.when(phase == 1)
    def _():
        core = at_ref[1]
        for j in range(per_step // 2):
            for ref, which in ((keep_ref, core), (send_ref, 1 - core)):
                term = dot(both[...], w_ref[2 * j + which, :, : 2 * ff], ((1,), (1,)))
                ref[j, :, : 2 * width] = (term * scale[...]).astype(BF16)
                ref[j, :, 2 * width :] = jnp.zeros((slots, ref.shape[2] - 2 * width), BF16)


def router_kernel(experts, at_ref, gates_ref, chance_ref, slots_ref, score_ref, part_ref):
    gate = jnp.sum(gates_ref[...], axis=0, keepdims=True)
    chances = chance_ref[...]
    own = (lax.broadcasted_iota(jnp.int32, chances.shape, 0) == at_ref[0]).astype(F32)
    gating = jnp.sum(chances * own, axis=0, keepdims=True)
    score = ((gate * gating) * (own - chances)).astype(BF16)
    score_ref[...] = score
    part_ref[...] = dot(score, slots_ref[...])[:, : part_ref.shape[1]]


def fits(rows, capacity, per_row):
    row = lax.broadcasted_iota(jnp.int32, (rows, 128), 0) & (capacity - 1)
    lane = lax.broadcasted_iota(jnp.int32, (rows, 128), 1)
    return (lane >= row * per_row) & (lane < row * per_row + per_row)


def return_kernel(
    capacity, per_row, sums_ref, score_ref, router_ref, column_ref, fold_ref, out_ref
):
    rows = sums_ref.shape[0]
    width = router_ref.shape[1]
    back = dot(score_ref[...], router_ref[...], ((0,), (0,)))
    out_ref[:, :width] = (sums_ref[:, :width].astype(F32) + back).astype(BF16)
    column = jnp.sum(column_ref[...], axis=0, keepdims=True)
    high = column.astype(BF16)
    low = (column - high.astype(F32)).astype(BF16)
    mask = fits(rows, capacity, per_row)
    spread = [jnp.where(mask, part.astype(F32), 0.0).astype(BF16) for part in (high, low)]
    folded = dot(spread[0], fold_ref[0]) + dot(spread[1], fold_ref[1])
    out_ref[:, width:] = folded.astype(BF16)


def combine_kernel(
    capacity, per_row, got_ref, pick_ref, fold_ref, mixed_ref, token_ref, router_ref
):
    rows = got_ref.shape[0]
    width = mixed_ref.shape[1]
    pair = dot(pick_ref[...], got_ref[:, : 2 * width])
    token_ref[...] = pair[:, :width].astype(BF16)
    mixed_ref[...] = pair[:, width:].astype(BF16)
    tail = got_ref[:, 2 * width :]
    spread = dot(tail, fold_ref[0], ((1,), (1,))) + dot(tail, fold_ref[1], ((1,), (1,)))
    spread = jnp.where(fits(rows, capacity, per_row), spread, 0.0)
    columns = jnp.sum(spread.reshape(rows // capacity, capacity, 128), axis=1)
    router_ref[...] = columns.T[: router_ref.shape[0]]


def shards(tokens, cotangent, routes, router, w_in, w_out):
    tok_count, width = tokens.shape
    experts = router.shape[1]
    sources = lax.axis_size("expert")
    groups = lax.axis_size("dp")
    chips = groups // 2
    capacity = 8
    slots = sources * capacity
    ff = w_in.shape[2]
    tail = 48
    per_row = width // capacity
    same_core = [[2 * chip + core for chip in range(chips)] for core in range(2)]
    swap = [(index, index ^ 1) for index in range(groups)]
    dp = lax.axis_index("dp")
    at = jnp.stack([lax.axis_index("expert"), dp % 2]).astype(jnp.int32)
    fold = np.zeros((2, 128, tail), np.float32)
    for lane in range(width):
        fold[0, lane, lane % per_row] = 1
        fold[1, lane, per_row + lane % per_row] = 1
    fold = jnp.asarray(fold, BF16)

    mine, pick = call(
        functools.partial(place_kernel, capacity, experts),
        (
            jax.ShapeDtypeStruct((slots, 2 * width), BF16),
            jax.ShapeDtypeStruct((tok_count, slots), BF16),
        ),
        [VMEM] * 3,
    )(routes, tokens, cotangent)
    got = lax.all_to_all(
        mine.reshape(sources, capacity, 2 * width), "expert", split_axis=0, concat_axis=0, tiled=True
    ).reshape(slots, 2 * width)

    got, w_in, w_out, router = lax.optimization_barrier((got, w_in, w_out, router))
    whole = lax.all_gather(got[None], "dp", axis=0, tiled=True)

    front = w_in[0].reshape(groups, width, ff)
    back = w_out[0].T.reshape(groups, width, ff)
    gate_rows = jnp.pad(router.reshape(groups, width, experts), ((0, 0), (0, 0), (0, 128 - experts)))
    empty = jnp.zeros_like(front)
    weights = jnp.concatenate(
        [
            jnp.concatenate([front, empty, gate_rows], axis=2),
            jnp.concatenate([empty, back, jnp.zeros_like(gate_rows)], axis=2),
        ],
        axis=1,
    )

    per_step = 4
    steps = groups // per_step
    columns = 2 * ff + 128
    keep, send, gate_term, chances = pl.pallas_call(
        functools.partial(expert_kernel, ff, experts),
        grid_spec=pltpu.PrefetchScalarGridSpec(
            num_scalar_prefetch=1,
            grid=(2, steps),
            in_specs=[
                pl.BlockSpec(
                    (per_step, slots, 2 * width), lambda p, i, at: (i * (1 - p) + (steps - 1) * p, 0, 0)
                ),
                pl.BlockSpec((per_step, 2 * width, columns), lambda p, i, at: (i, 0, 0)),
            ],
            out_specs=[
                pl.BlockSpec((per_step // 2, slots, 256), lambda p, i, at: (i * p, 0, 0)),
                pl.BlockSpec((per_step // 2, slots, 256), lambda p, i, at: (i * p, 0, 0)),
                pl.BlockSpec((8, slots), lambda p, i, at: (0, 0)),
                pl.BlockSpec((experts, slots), lambda p, i, at: (0, 0)),
            ],
            scratch_shapes=[
                pltpu.VMEM((slots, columns), F32),
                pltpu.VMEM((slots, 2 * ff), BF16),
                pltpu.VMEM((slots, 2 * width), F32),
            ],
        ),
        out_shape=(
            jax.ShapeDtypeStruct((chips, slots, 256), BF16),
            jax.ShapeDtypeStruct((chips, slots, 256), BF16),
            jax.ShapeDtypeStruct((8, slots), F32),
            jax.ShapeDtypeStruct((experts, slots), F32),
        ),
        compiler_params=pltpu.CompilerParams(vmem_limit_bytes=VMEM_LIMIT),
        cost_estimate=pl.CostEstimate(
            flops=8_000_000_000, bytes_accessed=24_000_000, transcendentals=slots * ff
        ),
    )(at, whole, weights)

    swapped = lax.ppermute(send, "dp", swap)
    halves = (keep.astype(F32) + swapped.astype(F32)).astype(BF16)
    sums = lax.psum_scatter(
        halves, "dp", scatter_dimension=0, axis_index_groups=same_core, tiled=True
    )

    gates = lax.all_to_all(
        jnp.broadcast_to(gate_term[None, :1], (groups, 1, slots)),
        "dp",
        split_axis=0,
        concat_axis=0,
        tiled=True,
    ).reshape(groups, slots)
    score_grad, router_part = call(
        functools.partial(router_kernel, experts),
        (
            jax.ShapeDtypeStruct((experts, slots), BF16),
            jax.ShapeDtypeStruct((experts, 128), F32),
        ),
        [SMEM] + [VMEM] * 3,
    )(at, gates, chances, got)
    router_column = lax.all_to_all(
        router_part.reshape(experts, 1, 128), "expert", split_axis=0, concat_axis=0, tiled=True
    ).reshape(experts, 128)

    router_slice = lax.dynamic_slice_in_dim(router, dp * width, width, 0).T
    router_slice = jnp.pad(router_slice, ((0, 0), (0, width)))
    home = call(
        functools.partial(return_kernel, capacity, per_row),
        jax.ShapeDtypeStruct((slots, 2 * width + tail), BF16),
        [VMEM] * 5,
    )(sums.reshape(slots, 256), score_grad, router_slice, router_column, fold)
    home = lax.all_to_all(
        home.reshape(sources, capacity, 2 * width + tail),
        "expert",
        split_axis=0,
        concat_axis=0,
        tiled=True,
    ).reshape(slots, 2 * width + tail)
    mixed, token_grad, router_grad = call(
        functools.partial(combine_kernel, capacity, per_row),
        (
            jax.ShapeDtypeStruct((tok_count, width), BF16),
            jax.ShapeDtypeStruct((tok_count, width), BF16),
            jax.ShapeDtypeStruct((width, experts), F32),
        ),
        [VMEM] * 3,
    )(home, pick, fold)
    return (mixed, token_grad, router_grad)


def solution(mesh):
    placed = (
        P("expert", "dp"),
        P("expert", "dp"),
        P("expert", None),
        P(),
        P("expert", None, "dp"),
        P("expert", "dp", None),
    )
    return jax.shard_map(
        shards,
        mesh=mesh,
        in_specs=placed,
        out_specs=(P("expert", "dp"), P("expert", "dp"), P("dp", None)),
        check_vma=False,
    )
```

time: 524 us -> 199 us (0.38)
  the two profiles are of different devices: /device:TPU:16 before, /device:TPU:6 now
where the time goes in v1:
time: 199 us; the launch traced here: 198 us
  blocking collectives  65.5 us (33%)
  waiting for transfers between devices  57.8 us (29%)
  starting transfers between devices  22 us (11%)
  Pallas kernels  20.3 us (10%)
  between operations  14.2 us (7%)
  local copies, waits for them, and re-layouts  11.3 us (6%)
  other arithmetic  7.47 us (4%)
    all_to_all x1, blocking collectives, shards(): lax.all_to_all(mine.reshape(sources, capacity, 2 * width), 'expert', spli...  38.3 us
    all_gather x1, waiting for transfers between devices, shards(): whole = lax.all_gather(got[None], 'dp', axis=0, tiled=True)  28.7 us
    all_to_all x1, blocking collectives, shards(): lax.all_to_all(home.reshape(sources, capacity, 2 * width + tail), 'expert...  27.2 us
    pallas_call x1, Pallas kernels, shards(): pl.pallas_call(functools.partial(expert_kernel, ff, experts), grid_spec=p...  17.4 us
    all_to_all x1, starting transfers between devices, shards(): lax.all_to_all(router_part.reshape(experts, 1, 128), 'expert', split_axis...  14 us
    all_to_all x1, waiting for transfers between devices, shards(): lax.all_to_all(router_part.reshape(experts, 1, 128), 'expert', split_axis...  11 us
    reduce_scatter x1, waiting for transfers between devices, shards(): lax.psum_scatter(halves, 'dp', scatter_dimension=0, axis_index_groups=sam...  9.47 us
    all_to_all x1, starting transfers between devices, shards(): lax.all_to_all(jnp.broadcast_to(gate_term[None, :1], (groups, 1, slots)),...  5.65 us
  transfers between devices with their start and end apart: 5, of which 5 were waited for; matrix products, arithmetic and copies ran while one was open for 6% of the time, Pallas kernels for 1%

profile of v1, /device:TPU:6, one launch (start us, length us, event | category | flops | bytes accessed | tf_op | source)
XLA Modules:
  0.0 198.4 jit_solution(9073033941915593012)
XLA Ops:
  7.2 0.0 all-gather.3.cloned.1.call-start
  7.2 0.8 copy.18.routes_ref
  8.0 0.8 copy.19.tok_ref
  8.8 0.9 copy.20.cot_ref
  9.7 0.7 shard_map.94
  10.5 38.3 %all_to_all.20 = bf16[64,8,208]{2,1,0:T(8,128)(2,1)} all-to-all(bf16[64,8,208]{2,1,0:T(8,128)(2,1)S(1)} %bitcast.28), channel_id=1, replica_groups=mesh['expert'=64,'dp'=16] {'expert'}, dimensions={0} | all-to-all | bytes 425984 | tf_op jit(solution)/shard_map/all_to_all | solution.py:212
  48.8 0.0 all-gather.3.cloned.1.call-update
  48.8 0.0 reduce-scatter.2.cloned.1.call-start
  48.9 0.1 pad_add_fusion.at_ref
  49.0 1.2 copy.21
  50.2 2.8 %copy.22 = bf16[1664,512]{1,0:T(8,128)(2,1)S(1)} copy(bf16[1664,512]{0,1:T(8,128)(2,1)} %bitcast.34) | data formatting | bytes 3407872 | tf_op jit(solution)/shard_map/transpose | solution.py:220
  53.0 0.1 broadcast_in_dim.18
  53.1 5.6 %fusion.4.w_ref = bf16[16,208,1152]{2,1,0:T(8,128)(2,1)} fusion(bf16[16,104,64]{2,1,0:T(8,128)(2,1)S(1)} %bitcast.35, bf16[16,104,512]{2,1,0:T(8,128)(2,1)S(1)} %bitcast.32, bf16[16,104,512]{2,1,0:T(8,128)(2,1)S(1)} %broadcast_in_dim.18, bf16[16,104,512]{2,1,0:T(8,128)(2,1)} %bitcast.33, bf16[208,1152]{1,0:T(8,128)(2,1)S(1)} %pad.15.clone), kind=kLoop, calls=%fused_computation.6 | loop fusion | flops 65175552 | bytes 13471744 | tf_op jit(solution)/shard_map/concatenate | solution.py:223
  58.7 28.7 %all-gather.3.cloned.1.call-done = bf16[8192,208]{1,0:T(8,128)(2,1)} async-done(((bf16[512,208]{1,0:T(8,128)(2,1)}), bf16[8192,208]{1,0:T(8,128)(2,1)}) %all-gather.3.cloned.1.call-update) | async-done | bytes 3407888 | tf_op jit(solution)/shard_map/all_gather | solution.py:217
  87.4 17.4 %shard_map.95 = (bf16[8,512,256]{2,1,0:T(8,128)(2,1)S(1)}, bf16[8,512,256]{2,1,0:T(8,128)(2,1)S(1)}, f32[8,512]{1,0:T(8,128)S(1)}, f32[64,512]{1,0:T(8,128)S(1)}) custom-call(s32[2]{0:T(128)S(1)} %pad_add_fusion.at_ref, bf16[16,512,208]{2,1,0:T(8,128)(2,1)} %bitcast.37, bf16[16,208,1152]{2,1,0:T(8,128)(2,1)} %fusion.4.w_ref), custom_call_target="tpu_custom_call" | custom-call | flops 8000000000 | bytes 24000000 | tf_op jit(solution)/shard_map/pallas_call | solution.py:234
  104.8 0.0 copy-start
  104.9 0.0 copy-start.2
  104.9 2.3 %collective-permute-start = (bf16[8,512,256]{2,1,0:T(8,128)(2,1)S(1)}, bf16[8,512,256]{2,1,0:T(8,128)(2,1)S(1)}, u32[]{:S(2)}, u32[]{:S(2)}) collective-permute-start(bf16[8,512,256]{2,1,0:T(8,128)(2,1)S(1)} %get-tuple-element.21), channel_id=1, source_target_pairs={{0,1},{1,0},{2,3},{3,2},{4,5},{5,4},{6,7},{7,6},{8,9},{9,8},{10,11... | collective-permute-start | bytes 6291464 | tf_op jit(solution)/shard_map/ppermute | solution.py:269
  107.2 3.9 %collective-permute-done = bf16[8,512,256]{2,1,0:T(8,128)(2,1)S(1)} collective-permute-done((bf16[8,512,256]{2,1,0:T(8,128)(2,1)S(1)}, bf16[8,512,256]{2,1,0:T(8,128)(2,1)S(1)}, u32[]{:S(2)}, u32[]{:S(2)}) %collective-permute-start) | collective-permute-done | bytes 2097184 | tf_op jit(solution)/shard_map/ppermute | solution.py:269
  111.1 1.8 add_convert_fusion
  112.9 0.0 reduce-scatter.2.cloned.1.call-update
  112.9 0.6 broadcast_in_dim.21
  113.6 5.7 %all-to-all-start.1 = ((f32[16,1,512]{2,1,0:T(1,128)}), f32[16,1,512]{2,1,0:T(1,128)S(1)}, u32[]{:S(2)}, u32[]{:S(2)}) async-start(f32[16,1,512]{2,1,0:T(1,128)} %broadcast_in_dim.21), calls=%async_computation.2 | async-start | bytes 65536 | tf_op jit(solution)/shard_map/all_to_all | solution.py:275
  119.2 4.6 %all-to-all-done.1 = f32[16,1,512]{2,1,0:T(1,128)S(1)} async-done(((f32[16,1,512]{2,1,0:T(1,128)}), f32[16,1,512]{2,1,0:T(1,128)S(1)}, u32[]{:S(2)}, u32[]{:S(2)}) %all-to-all-start.1) | async-done | bytes 32800 | tf_op jit(solution)/shard_map/all_to_all | solution.py:275
  123.8 0.0 copy-done
  123.8 1.3 shard_map.96
  125.2 14.0 %all-to-all-start.2 = ((f32[64,1,128]{2,1,0:T(1,128)}), f32[64,1,128]{2,1,0:T(1,128)S(1)}, u32[]{:S(2)}, u32[]{:S(2)}) async-start(f32[64,1,128]{2,1,0:T(1,128)} %bitcast.14), calls=%async_computation.3 | async-start | bytes 65536 | tf_op jit(solution)/shard_map/all_to_all | solution.py:290
  139.2 0.8 dynamic-slice_bitcast_fusion
  140.0 11.0 %all-to-all-done.2 = f32[64,1,128]{2,1,0:T(1,128)S(1)} async-done(((f32[64,1,128]{2,1,0:T(1,128)}), f32[64,1,128]{2,1,0:T(1,128)S(1)}, u32[]{:S(2)}, u32[]{:S(2)}) %all-to-all-start.2) | async-done | bytes 32800 | tf_op jit(solution)/shard_map/all_to_all | solution.py:290
  151.0 9.5 %reduce-scatter.2.cloned.1.call-done = bf16[1,512,256]{2,1,0:T(8,128)(2,1)} async-done(((bf16[8,512,256]{2,1,0:T(8,128)(2,1)}), bf16[1,512,256]{2,1,0:T(8,128)(2,1)}) %reduce-scatter.2.cloned.1.call-update) | async-done | bytes 262160 | tf_op jit(solution)/shard_map/reduce_scatter | solution.py:271
  160.5 0.0 copy-done.2
  160.5 0.0 copy-start.1
  160.5 0.9 copy-done.1
  161.5 0.4 shard_map.97
  161.9 27.2 %all_to_all.21 = bf16[64,8,256]{2,1,0:T(8,128)(2,1)S(1)} all-to-all(bf16[64,8,256]{2,1,0:T(8,128)(2,1)S(1)} %bitcast.27), channel_id=1, replica_groups=mesh['expert'=64,'dp'=16] {'expert'}, dimensions={0} | all-to-all | bytes 524288 | tf_op jit(solution)/shard_map/all_to_all | solution.py:301
  189.1 0.4 shard_map.98
  189.5 0.7 copy.26
  190.2 0.7 copy.24
  190.9 0.7 copy.25
  (5 shorter events, 0.1 us)
Async XLA Ops:
  7.2 80.3 %all-gather.3.cloned.1.call-start = ((), (), s32[]{:S(2)}) async-start(), calls=%async_computation.6 | async-start | bytes 4456448 | tf_op jit(solution)/shard_map/all_gather | solution.py:217
  48.8 111.7 %reduce-scatter.2.cloned.1.call-start = ((), (), s32[]{:S(2)}) async-start(), calls=%async_computation.5 | async-start | bytes 2359296 | tf_op jit(solution)/shard_map/reduce_scatter | solution.py:271
  104.8 19.0 %copy-start = (bf16[64,8,208]{2,1,0:T(8,128)(2,1)S(1)}, bf16[64,8,208]{2,1,0:T(8,128)(2,1)}, u32[]{:S(2)}) copy-start(bf16[64,8,208]{2,1,0:T(8,128)(2,1)} %all_to_all.20) | copy-start | bytes 638980
  104.9 55.7 %copy-start.2 = (bf16[2,128,48]{2,1,0:T(8,128)(2,1)S(1)}, bf16[2,128,48]{2,1,0:T(8,128)(2,1)}, u32[]{:S(2)}) copy-start(bf16[2,128,48]{2,1,0:T(8,128)(2,1)} %constant.33.clone.fold_ref) | copy-start | bytes 73732
  104.9 6.2 %collective-permute-start = (bf16[8,512,256]{2,1,0:T(8,128)(2,1)S(1)}, bf16[8,512,256]{2,1,0:T(8,128)(2,1)S(1)}, u32[]{:S(2)}, u32[]{:S(2)}) collective-permute-start(bf16[8,512,256]{2,1,0:T(8,128)(2,1)S(1)} %get-tuple-element.21), channel_id=1, source_target_pairs={{0,1},{1,0},{2,3},{3,2},{4,5},{5,4},{6,7},{7,6},{8,9},{9,8},{10,11... | collective-permute-start | bytes 6291464 | tf_op jit(solution)/shard_map/ppermute | solution.py:269
  113.6 10.3 %all-to-all-start.1 = ((f32[16,1,512]{2,1,0:T(1,128)}), f32[16,1,512]{2,1,0:T(1,128)S(1)}, u32[]{:S(2)}, u32[]{:S(2)}) async-start(f32[16,1,512]{2,1,0:T(1,128)} %broadcast_in_dim.21), calls=%async_computation.2 | async-start | bytes 65536 | tf_op jit(solution)/shard_map/all_to_all | solution.py:275
  125.2 25.9 %all-to-all-start.2 = ((f32[64,1,128]{2,1,0:T(1,128)}), f32[64,1,128]{2,1,0:T(1,128)S(1)}, u32[]{:S(2)}, u32[]{:S(2)}) async-start(f32[64,1,128]{2,1,0:T(1,128)} %bitcast.14), calls=%async_computation.3 | async-start | bytes 65536 | tf_op jit(solution)/shard_map/all_to_all | solution.py:290
  160.5 1.0 copy-start.1
Sparse Core Ops, SparseCore 0:
  48.9 38.4 all-gather.2
  113.0 47.4 reduce-scatter.1

commit v2 on v1

v2 whole, which is shorter than its diff:
```python
import functools

import jax
import jax.numpy as jnp
import numpy as np
from jax import lax
from jax.experimental import pallas as pl
from jax.experimental.pallas import tpu as pltpu
from jax.sharding import PartitionSpec as P

F32 = jnp.float32
BF16 = jnp.bfloat16
LANES = 128
VMEM_LIMIT = 48 * 1024 * 1024
VMEM = pl.BlockSpec(memory_space=pltpu.VMEM)
SMEM = pl.BlockSpec(memory_space=pltpu.SMEM)


def dot(a, b, dims=((1,), (0,))):
    return lax.dot_general(a, b, (dims, ((), ())), preferred_element_type=F32)


def call(body, out_shape, in_specs, flops=10_000_000, moved=1_000_000):
    return pl.pallas_call(
        body,
        out_shape=out_shape,
        in_specs=in_specs,
        out_specs=jax.tree.map(lambda _: VMEM, out_shape),
        compiler_params=pltpu.CompilerParams(vmem_limit_bytes=VMEM_LIMIT),
        cost_estimate=pl.CostEstimate(flops=flops, bytes_accessed=moved, transcendentals=0),
    )


def place_kernel(capacity, experts, routes_ref, tok_ref, cot_ref, slots_ref, pick_ref):
    width, rows = tok_ref.shape
    slots = slots_ref.shape[0]
    routes = routes_ref[...]
    number = lax.broadcasted_iota(jnp.int32, (experts, rows), 0)
    hot = [(routes[k : k + 1] == number).astype(F32) for k in range(2)]
    before = lax.broadcasted_iota(jnp.int32, (rows, rows), 0) < lax.broadcasted_iota(
        jnp.int32, (rows, rows), 1
    )
    before = before.astype(F32).astype(BF16)
    first = dot(hot[0].astype(BF16), before)
    second = dot(hot[1].astype(BF16), before) + jnp.sum(hot[0], axis=1, keepdims=True)
    rank = [
        jnp.sum(first * hot[0], axis=0, keepdims=True),
        jnp.sum(second * hot[1], axis=0, keepdims=True),
    ]
    place = lax.broadcasted_iota(jnp.int32, (slots, rows), 0)
    target = [routes[k : k + 1] * capacity + rank[k].astype(jnp.int32) for k in range(2)]
    pick = ((place == target[0]) | (place == target[1])).astype(F32).astype(BF16)
    pick_ref[...] = pick
    blank = jnp.zeros((slots, LANES - width), BF16)
    for at, ref in ((0, tok_ref), (LANES, cot_ref)):
        slots_ref[:, at : at + width] = dot(pick, ref[...], ((1,), (1,))).astype(BF16)
        slots_ref[:, at + width : at + LANES] = blank


def terms(pre, hidden, gating, front_ref, back_ref, which, out_ref):
    pairs = out_ref.shape[0]
    offsets = [pl.multiple_of((2 * j + which) * LANES, LANES) for j in range(pairs)]
    front = jnp.concatenate([front_ref[pl.ds(at, LANES), :] for at in offsets], axis=0)
    back = jnp.concatenate([back_ref[:, pl.ds(at, LANES)] for at in offsets], axis=1)
    grad = dot(pre, front, ((1,), (1,)))
    out = dot(hidden, back)
    for j in range(pairs):
        lanes = slice(j * LANES, (j + 1) * LANES)
        out_ref[j, :, :LANES] = grad[:, lanes].astype(BF16)
        out_ref[j, :, LANES:] = (gating * out[:, lanes]).astype(BF16)


def expert_kernel(
    experts,
    at_ref,
    got_ref,
    front_ref,
    back_ref,
    router_ref,
    send_ref,
    pre_ref,
    hidden_ref,
    gating_ref,
    gate_ref,
    chance_ref,
    acc,
    proj,
    rates,
):
    phase, step = pl.program_id(0), pl.program_id(1)
    per_step, slots = got_ref.shape[0], got_ref.shape[1]

    @pl.when(phase == 0)
    def _():
        tok = jnp.concatenate([got_ref[j, :, :LANES] for j in range(per_step)], axis=1)
        cot = jnp.concatenate([got_ref[j, :, LANES:] for j in range(per_step)], axis=1)

        @pl.when(step == 0)
        def _():
            acc[...] = dot(tok, front_ref[...])
            proj[...] = dot(cot, back_ref[...], ((1,), (1,)))
            rates[...] = dot(tok, router_ref[...], ((1,), (1,)))

        @pl.when(step > 0)
        def _():
            acc[...] += dot(tok, front_ref[...])
            proj[...] += dot(cot, back_ref[...], ((1,), (1,)))
            rates[...] += dot(tok, router_ref[...], ((1,), (1,)))

    @pl.when((phase == 0) & (step == pl.num_programs(1) - 1))
    def _():
        chunk = 64
        own = at_ref[0]

        def one(i, carry):
            rows = pl.ds(pl.multiple_of(i * chunk, chunk), chunk)
            scores = rates[rows, :]
            lane = lax.broadcasted_iota(jnp.int32, scores.shape, 1)
            scores = jnp.where(lane < experts, scores, -jnp.inf)
            top = jnp.max(scores, axis=1, keepdims=True)
            raised = jnp.exp(scores - top)
            chances = raised / jnp.sum(raised, axis=1, keepdims=True)
            gating = jnp.sum(jnp.where(lane == own, chances, 0.0), axis=1, keepdims=True)
            x = acc[rows, :]
            up = proj[rows, :]
            c = np.float32(np.sqrt(2.0 / np.pi))
            square = x * x
            t = jnp.tanh(c * (x + 0.044715 * (square * x)))
            half = 0.5 * (1.0 + t)
            hidden = (x * half).astype(BF16)
            slope = half + 0.5 * x * (1.0 - t * t) * (c * (1.0 + 3 * 0.044715 * square))
            pre_ref[rows, :] = (slope * (gating * up)).astype(BF16)
            hidden_ref[rows, :] = hidden
            gate = jnp.sum(hidden.astype(F32) * up, axis=1, keepdims=True)
            rates[rows, :] = jnp.where(lane == experts, gate, chances)
            gating_ref[rows, :] = jnp.broadcast_to(gating, (chunk, LANES))
            return carry

        lax.fori_loop(0, slots // chunk, one, 0)
        turned = rates[...].T
        chance_ref[...] = turned[:experts]
        gate_ref[...] = turned[experts : experts + 8]

    @pl.when(phase == 1)
    def _():
        terms(
            pre_ref[...], hidden_ref[...], gating_ref[...], front_ref, back_ref, 1 - at_ref[1], send_ref
        )


def keep_kernel(at_ref, pre_ref, hidden_ref, gating_ref, front_ref, back_ref, keep_ref):
    terms(pre_ref[...], hidden_ref[...], gating_ref[...], front_ref, back_ref, at_ref[1], keep_ref)


def router_kernel(at_ref, gates_ref, chance_ref, slots_ref, score_ref, part_ref):
    gate = jnp.sum(gates_ref[...], axis=0, keepdims=True)
    chances = chance_ref[...]
    own = (lax.broadcasted_iota(jnp.int32, chances.shape, 0) == at_ref[0]).astype(F32)
    gating = jnp.sum(chances * own, axis=0, keepdims=True)
    score = ((gate * gating) * (own - chances)).astype(BF16)
    score_ref[...] = score
    part_ref[...] = dot(score, slots_ref[:, :LANES])


def fits(rows, capacity, per_row):
    row = lax.broadcasted_iota(jnp.int32, (rows, LANES), 0) & (capacity - 1)
    lane = lax.broadcasted_iota(jnp.int32, (rows, LANES), 1)
    return (lane >= row * per_row) & (lane < row * per_row + per_row)


def return_kernel(
    capacity, per_row, sums_ref, score_ref, router_ref, column_ref, fold_ref, out_ref
):
    rows = sums_ref.shape[0]
    back = dot(score_ref[...], router_ref[...], ((0,), (0,)))
    column = jnp.sum(column_ref[...], axis=0, keepdims=True)
    high = column.astype(BF16)
    low = (column - high.astype(F32)).astype(BF16)
    mask = fits(rows, capacity, per_row)
    high, low = [
        dot(jnp.where(mask, part.astype(F32), 0.0).astype(BF16), fold_ref[...]) for part in (high, low)
    ]
    sums = sums_ref[...].astype(F32)
    out_ref[:, :LANES] = (sums[:, :LANES] + back + high).astype(BF16)
    out_ref[:, LANES:] = (sums[:, LANES:] + low).astype(BF16)


def combine_kernel(
    capacity, per_row, got_ref, pick_ref, fold_ref, mixed_ref, token_ref, router_ref
):
    rows = got_ref.shape[0]
    width = mixed_ref.shape[0]
    got = got_ref[...]
    pair = dot(got, pick_ref[...], ((0,), (0,)))
    token_ref[...] = pair[:width].astype(BF16)
    mixed_ref[...] = pair[LANES : LANES + width].astype(BF16)
    spread = [dot(part, fold_ref[...], ((1,), (1,))) for part in (got[:, :LANES], got[:, LANES:])]
    spread = jnp.where(fits(rows, capacity, per_row), spread[0] + spread[1], 0.0)
    columns = jnp.sum(spread.reshape(rows // capacity, capacity, LANES), axis=1)
    router_ref[...] = columns[:, : router_ref.shape[1]]


def shards(tokens, cotangent, routes, router, w_in, w_out):
    tok_count, width = tokens.shape
    experts = router.shape[1]
    sources = lax.axis_size("expert")
    groups = lax.axis_size("dp")
    chips = groups // 2
    capacity = 8
    slots = sources * capacity
    ff = w_in.shape[2]
    lanes = 2 * LANES
    per_row = width // capacity
    same_core = [[2 * chip + core for chip in range(chips)] for core in range(2)]
    swap = [(index, index ^ 1) for index in range(groups)]
    dp = lax.axis_index("dp")
    at = jnp.stack([lax.axis_index("expert"), dp % 2]).astype(jnp.int32)
    fold = np.zeros((LANES, LANES), np.float32)
    for lane in range(width):
        fold[lane, width + lane % per_row] = 1
    fold = jnp.asarray(fold, BF16)

    mine, pick = call(
        functools.partial(place_kernel, capacity, experts),
        (
            jax.ShapeDtypeStruct((slots, lanes), BF16),
            jax.ShapeDtypeStruct((slots, tok_count), BF16),
        ),
        [VMEM] * 3,
    )(routes.T, tokens.T, cotangent.T)
    got = lax.all_to_all(
        mine.reshape(sources, capacity, lanes), "expert", split_axis=0, concat_axis=0, tiled=True
    ).reshape(slots, lanes)

    got, w_in, w_out, router = lax.optimization_barrier((got, w_in, w_out, router))
    whole = lax.all_gather(got[None], "dp", axis=0, tiled=True)

    spare = LANES - width
    front = jnp.pad(w_in[0].reshape(groups, width, ff), ((0, 0), (0, spare), (0, 0)))
    front = front.reshape(groups * LANES, ff)
    back = jnp.pad(w_out[0].reshape(ff, groups, width), ((0, 0), (0, 0), (0, spare)))
    back = back.reshape(ff, groups * LANES)
    scorer = jnp.pad(
        router.T.reshape(experts, groups, width), ((0, LANES - experts), (0, 0), (0, spare))
    ).reshape(LANES, groups * LANES)

    per_step = 4
    steps = groups // per_step
    depth = per_step * LANES
    send, pre, hidden, gating, gate_term, chances = pl.pallas_call(
        functools.partial(expert_kernel, experts),
        grid_spec=pltpu.PrefetchScalarGridSpec(
            num_scalar_prefetch=1,
            grid=(2, steps),
            in_specs=[
                pl.BlockSpec(
                    (per_step, slots, lanes), lambda p, i, at: (i * (1 - p) + (steps - 1) * p, 0, 0)
                ),
                pl.BlockSpec((depth, ff), lambda p, i, at: (i, 0)),
                pl.BlockSpec((ff, depth), lambda p, i, at: (0, i)),
                pl.BlockSpec((LANES, depth), lambda p, i, at: (0, i * (1 - p) + (steps - 1) * p)),
            ],
            out_specs=[
                pl.BlockSpec((per_step // 2, slots, lanes), lambda p, i, at: (i * p, 0, 0)),
                pl.BlockSpec((slots, ff), lambda p, i, at: (0, 0)),
                pl.BlockSpec((slots, ff), lambda p, i, at: (0, 0)),
                pl.BlockSpec((slots, LANES), lambda p, i, at: (0, 0)),
                pl.BlockSpec((8, slots), lambda p, i, at: (0, 0)),
                pl.BlockSpec((experts, slots), lambda p, i, at: (0, 0)),
            ],
            scratch_shapes=[
                pltpu.VMEM((slots, ff), F32),
                pltpu.VMEM((slots, ff), F32),
                pltpu.VMEM((slots, LANES), F32),
            ],
        ),
        out_shape=(
            jax.ShapeDtypeStruct((chips, slots, lanes), BF16),
            jax.ShapeDtypeStruct((slots, ff), BF16),
            jax.ShapeDtypeStruct((slots, ff), BF16),
            jax.ShapeDtypeStruct((slots, LANES), F32),
            jax.ShapeDtypeStruct((8, slots), F32),
            jax.ShapeDtypeStruct((experts, slots), F32),
        ),
        compiler_params=pltpu.CompilerParams(vmem_limit_bytes=VMEM_LIMIT),
        cost_estimate=pl.CostEstimate(
            flops=4_000_000_000, bytes_accessed=16_000_000, transcendentals=slots * ff
        ),
    )(at, whole, front, back, scorer)

    swapped = lax.ppermute(send, "dp", swap)
    keep = pl.pallas_call(
        keep_kernel,
        grid_spec=pltpu.PrefetchScalarGridSpec(
            num_scalar_prefetch=1,
            grid=(steps,),
            in_specs=[
                pl.BlockSpec((slots, ff), lambda i, at: (0, 0)),
                pl.BlockSpec((slots, ff), lambda i, at: (0, 0)),
                pl.BlockSpec((slots, LANES), lambda i, at: (0, 0)),
                pl.BlockSpec((depth, ff), lambda i, at: (i, 0)),
                pl.BlockSpec((ff, depth), lambda i, at: (0, i)),
            ],
            out_specs=pl.BlockSpec((per_step // 2, slots, lanes), lambda i, at: (i, 0, 0)),
        ),
        out_shape=jax.ShapeDtypeStruct((chips, slots, lanes), BF16),
        compiler_params=pltpu.CompilerParams(vmem_limit_bytes=VMEM_LIMIT),
        cost_estimate=pl.CostEstimate(
            flops=2_000_000_000, bytes_accessed=8_000_000, transcendentals=0
        ),
    )(at, pre, hidden, gating, front, back)
    halves = (keep.astype(F32) + swapped.astype(F32)).astype(BF16)
    halves, gate_term = lax.optimization_barrier((halves, gate_term))
    sums = lax.psum_scatter(
        halves, "dp", scatter_dimension=0, axis_index_groups=same_core, tiled=True
    )

    gates = lax.all_to_all(
        jnp.broadcast_to(gate_term[None, :1], (groups, 1, slots)),
        "dp",
        split_axis=0,
        concat_axis=0,
        tiled=True,
    ).reshape(groups, slots)
    score_grad, router_part = call(
        router_kernel,
        (
            jax.ShapeDtypeStruct((experts, slots), BF16),
            jax.ShapeDtypeStruct((experts, LANES), F32),
        ),
        [SMEM] + [VMEM] * 3,
    )(at, gates, chances, got)
    router_column = lax.all_to_all(
        router_part.reshape(experts, 1, LANES), "expert", split_axis=0, concat_axis=0, tiled=True
    ).reshape(experts, LANES)

    router_slice = lax.dynamic_slice_in_dim(router.T, dp * width, width, 1)
    router_slice = jnp.pad(router_slice, ((0, 0), (0, spare)))
    home = call(
        functools.partial(return_kernel, capacity, per_row),
        jax.ShapeDtypeStruct((slots, lanes), BF16),
        [VMEM] * 5,
    )(sums.reshape(slots, lanes), score_grad, router_slice, router_column, fold)
    home = lax.all_to_all(
        home.reshape(sources, capacity, lanes), "expert", split_axis=0, concat_axis=0, tiled=True
    ).reshape(slots, lanes)
    mixed, token_grad, router_grad = call(
        functools.partial(combine_kernel, capacity, per_row),
        (
            jax.ShapeDtypeStruct((width, tok_count), BF16),
            jax.ShapeDtypeStruct((width, tok_count), BF16),
            jax.ShapeDtypeStruct((experts, width), F32),
        ),
        [VMEM] * 3,
    )(home, pick, fold)
    return (mixed.T, token_grad.T, router_grad.T)


def solution(mesh):
    placed = (
        P("expert", "dp"),
        P("expert", "dp"),
        P("expert", None),
        P(),
        P("expert", None, "dp"),
        P("expert", "dp", None),
    )
    return jax.shard_map(
        shards,
        mesh=mesh,
        in_specs=placed,
        out_specs=(P("expert", "dp"), P("expert", "dp"), P("dp", None)),
        check_vma=False,
    )
```

time: 199 us -> 191 us (0.960)
  other arithmetic: 7.47 us -> 1.92 us
  waiting for transfers between devices: 57.8 us -> 53.9 us
  local copies, waits for them, and re-layouts: 11.3 us -> 14.2 us
    concatenate x1 -> x0, other arithmetic: 5.56 us -> none  [shards(): jnp.concatenate([jnp.concatenate([front, empty, gate_rows], axis=2), jnp....]
    ppermute x1, waiting for transfers between devices: 3.9 us -> 0.01 us  [shards(): swapped = lax.ppermute(send, 'dp', swap)]
    transpose x2 -> x0, local copies, waits for them, and re-layouts: 3.68 us -> none  [the longest x1 2.84 us: shards(): back = w_out[0].T.reshape(groups, width, ff)]
    pad x1 -> x4, local copies, waits for them, and re-layouts: 0.01 us -> 3.6 us  [the longest x1 1.86 us: shards(): jnp.pad(w_in[0].reshape(groups, width, ff), ((0, 0), (0, spare), (0, 0)))]
    reshape x0 -> x2, local copies, waits for them, and re-layouts: none -> 3.03 us  [the longest x1 2.5 us: shards(): back = back.reshape(ff, groups * LANES)]
    optimization_barrier x1, local copies, waits for them, and re-layouts: 1.2 us -> 3.62 us  [shards(): lax.optimization_barrier((got, w_in, w_out, router))]
    pallas_call x3 -> x0, local copies, waits for them, and re-layouts: 2.12 us -> none  [shards(): call(functools.partial(combine_kernel, capacity, per_row), (jax.ShapeDtyp...]
    pallas_call x2 -> x3, Pallas kernels: 18.7 us -> 17 us  [the longest x1 11.5 us: shards(): pl.pallas_call(functools.partial(expert_kernel, experts), grid_spec=pltpu...]
  transfers between devices with their start and end apart: 5 -> 5, of which waited for: 5 -> 4; matrix products, arithmetic and copies ran while one was open for 6% -> 6% of each run, Pallas kernels for 1% -> 3%
where the time goes in v2:
time: 191 us; the launch traced here: 190 us
  blocking collectives  65.5 us (34%)
  waiting for transfers between devices  53.9 us (28%)
  starting transfers between devices  21.8 us (11%)
  Pallas kernels  18.6 us (10%)
  local copies, waits for them, and re-layouts  14.2 us (7%)
  between operations  14.2 us (7%)
  other arithmetic  1.92 us (1%)
    all_to_all x1, blocking collectives, shards(): lax.all_to_all(mine.reshape(sources, capacity, lanes), 'expert', split_ax...  38.3 us
    all_gather x1, waiting for transfers between devices, shards(): whole = lax.all_gather(got[None], 'dp', axis=0, tiled=True)  28.1 us
    all_to_all x1, blocking collectives, shards(): lax.all_to_all(home.reshape(sources, capacity, lanes), 'expert', split_ax...  27.2 us
    all_to_all x1, starting transfers between devices, shards(): lax.all_to_all(router_part.reshape(experts, 1, LANES), 'expert', split_ax...  14 us
    all_to_all x1, waiting for transfers between devices, shards(): lax.all_to_all(router_part.reshape(experts, 1, LANES), 'expert', split_ax...  11.8 us
    pallas_call x1, Pallas kernels, shards(): pl.pallas_call(functools.partial(expert_kernel, experts), grid_spec=pltpu...  11.5 us
    reduce_scatter x1, waiting for transfers between devices, shards(): lax.psum_scatter(halves, 'dp', scatter_dimension=0, axis_index_groups=sam...  9.38 us
    all_to_all x1, starting transfers between devices, shards(): lax.all_to_all(jnp.broadcast_to(gate_term[None, :1], (groups, 1, slots)),...  5.68 us
  transfers between devices with their start and end apart: 5, of which 4 were waited for; matrix products, arithmetic and copies ran while one was open for 6% of the time, Pallas kernels for 3%

profile of v2, /device:TPU:6, one launch (start us, length us, event | category | flops | bytes accessed | tf_op | source)
XLA Modules:
  0.0 190.2 jit_solution(10767077898197718448)
XLA Ops:
  7.2 0.0 all-gather.3.cloned.1.call-start
  7.2 0.0 copy-start.3
  7.2 0.7 copy-done.3
  8.0 0.0 copy-start.4
  8.0 0.7 copy-done.4
  8.7 0.0 copy-start.5
  8.7 0.7 copy-done.5
  9.4 0.4 shard_map.94
  9.7 38.3 %all_to_all.20 = bf16[64,8,256]{2,1,0:T(8,128)(2,1)} all-to-all(bf16[64,8,256]{2,1,0:T(8,128)(2,1)S(1)} %bitcast.40), channel_id=1, replica_groups=mesh['expert'=64,'dp'=16] {'expert'}, dimensions={0} | all-to-all | bytes 524288 | tf_op jit(solution)/shard_map/all_to_all | solution.py:231
  48.1 0.0 all-gather.3.cloned.1.call-update
  48.1 0.0 reduce-scatter.2.cloned.1.call-start
  48.1 0.1 pad_add_fusion.at_ref
  48.2 3.6 %copy.12 = bf16[1,512,1664]{1,2,0:T(8,128)(2,1)} copy(bf16[1,512,1664]{2,1,0:T(8,128)(2,1)} %param.12) | data formatting | bytes 3407872 | tf_op jit(solution)/shard_map/optimization_barrier | solution.py:235
  51.8 1.7 pad.17
  53.5 2.5 %copy.15.back_ref = bf16[512,2048]{1,0:T(8,128)(2,1)} copy(bf16[512,2048]{0,1:T(8,128)(2,1)S(1)} %bitcast.47) | data formatting | bytes 4194304 | tf_op jit(solution)/shard_map/reshape | solution.py:242
  56.0 0.0 copy-start.6
  56.0 1.9 pad.16
  57.9 0.0 copy-done.6
  57.9 0.5 reshape.49
  58.4 0.1 pad.18
  58.5 0.1 copy.20
  58.6 28.1 %all-gather.3.cloned.1.call-done = bf16[8192,256]{1,0:T(8,128)(2,1)} async-done(((bf16[512,256]{1,0:T(8,128)(2,1)}), bf16[8192,256]{1,0:T(8,128)(2,1)}) %all-gather.3.cloned.1.call-update) | async-done | bytes 4194320 | tf_op jit(solution)/shard_map/all_gather | solution.py:236
  86.7 11.5 %shard_map.95 = (bf16[8,512,256]{2,1,0:T(8,128)(2,1)S(1)}, bf16[512,512]{1,0:T(8,128)(2,1)S(1)}, bf16[512,512]{1,0:T(8,128)(2,1)S(1)}, f32[512,128]{1,0:T(8,128)...) custom-call(s32[2]{0:T(128)S(1)} %pad_add_fusion.at_ref, bf16[16,512,256]{2,1,0:T(8,128)(2,1)} %bitcast.53, ...), custom_call_target="tpu_custom_call" | custom-call | flops 4000000000 | bytes 16000000 | tf_op jit(solution)/shard_map/pallas_call | solution.py:250
  98.3 2.1 %collective-permute-start = (bf16[8,512,256]{2,1,0:T(8,128)(2,1)S(1)}, bf16[8,512,256]{2,1,0:T(8,128)(2,1)S(1)}, u32[]{:S(2)}, u32[]{:S(2)}) collective-permute-start(bf16[8,512,256]{2,1,0:T(8,128)(2,1)S(1)} %get-tuple-element.30), channel_id=1, source_target_pairs={{0,1},{1,0},{2,3},{3,2},{4,5},{5,4},{6,7},{7,6},{8,9},{9,8},{10,11... | collective-permute-start | bytes 6291464 | tf_op jit(solution)/shard_map/ppermute | solution.py:291
  100.4 4.1 %shard_map.96 = bf16[8,512,256]{2,1,0:T(8,128)(2,1)S(1)} custom-call(s32[2]{0:T(128)S(1)} %pad_add_fusion.at_ref, bf16[512,512]{1,0:T(8,128)(2,1)S(1)} %get-tuple-element.27.pre_ref, bf16[512,512]{1,0:T(8,128)(2,1)S(1)} %get-tuple-element.28.hidden_ref, f32[512,128]{1,0:T(8,128)S(1)} %get-tuple-element.29.gating_ref, bf16[2048,512]{1,0:T(8,128)(2,1)S(1)} %bitcast.34, ...), custom_call_target="tpu_custom_call" | custom-call | flops 2000000000 | bytes 8000000 | tf_op jit(solution)/shard_map/pallas_call | solution.py:292
  104.5 0.0 collective-permute-done
  104.5 1.8 add_convert_fusion
  106.4 0.0 copy-start
  106.4 0.0 copy-start.2
  106.4 0.0 reduce-scatter.2.cloned.1.call-update
  106.4 0.6 broadcast_in_dim.13
  107.0 5.7 %all-to-all-start.1 = ((f32[16,1,512]{2,1,0:T(1,128)}), f32[16,1,512]{2,1,0:T(1,128)S(1)}, u32[]{:S(2)}, u32[]{:S(2)}) async-start(f32[16,1,512]{2,1,0:T(1,128)} %broadcast_in_dim.13), calls=%async_computation.2 | async-start | bytes 65536 | tf_op jit(solution)/shard_map/all_to_all | solution.py:318
  112.7 4.6 %all-to-all-done.1 = f32[16,1,512]{2,1,0:T(1,128)S(1)} async-done(((f32[16,1,512]{2,1,0:T(1,128)}), f32[16,1,512]{2,1,0:T(1,128)S(1)}, u32[]{:S(2)}, u32[]{:S(2)}) %all-to-all-start.1) | async-done | bytes 32800 | tf_op jit(solution)/shard_map/all_to_all | solution.py:318
  117.3 0.0 copy-done
  117.3 1.3 shard_map.97
  118.7 14.0 %all-to-all-start.2 = ((f32[64,1,128]{2,1,0:T(1,128)}), f32[64,1,128]{2,1,0:T(1,128)S(1)}, u32[]{:S(2)}, u32[]{:S(2)}) async-start(f32[64,1,128]{2,1,0:T(1,128)} %bitcast.17), calls=%async_computation.3 | async-start | bytes 65536 | tf_op jit(solution)/shard_map/all_to_all | solution.py:333
  132.6 0.1 dynamic-slice_bitcast_fusion
  132.7 11.8 %all-to-all-done.2 = f32[64,1,128]{2,1,0:T(1,128)S(1)} async-done(((f32[64,1,128]{2,1,0:T(1,128)}), f32[64,1,128]{2,1,0:T(1,128)S(1)}, u32[]{:S(2)}, u32[]{:S(2)}) %all-to-all-start.2) | async-done | bytes 32800 | tf_op jit(solution)/shard_map/all_to_all | solution.py:333
  144.5 9.4 %reduce-scatter.2.cloned.1.call-done = bf16[1,512,256]{2,1,0:T(8,128)(2,1)} async-done(((bf16[8,512,256]{2,1,0:T(8,128)(2,1)}), bf16[1,512,256]{2,1,0:T(8,128)(2,1)}) %reduce-scatter.2.cloned.1.call-update) | async-done | bytes 262160 | tf_op jit(solution)/shard_map/reduce_scatter | solution.py:314
  153.9 0.0 copy-done.2
  153.9 0.0 copy-start.1
  153.9 0.9 copy-done.1
  154.9 0.3 shard_map.98
  155.2 27.2 %all_to_all.21 = bf16[64,8,256]{2,1,0:T(8,128)(2,1)S(1)} all-to-all(bf16[64,8,256]{2,1,0:T(8,128)(2,1)S(1)} %bitcast.38), channel_id=1, replica_groups=mesh['expert'=64,'dp'=16] {'expert'}, dimensions={0} | all-to-all | bytes 524288 | tf_op jit(solution)/shard_map/all_to_all | solution.py:344
  182.4 1.0 shard_map.99
  (3 shorter events, 0.0 us)
Async XLA Ops:
  7.2 79.6 %all-gather.3.cloned.1.call-start = ((), (), s32[]{:S(2)}) async-start(), calls=%async_computation.6 | async-start | bytes 4456448 | tf_op jit(solution)/shard_map/all_gather | solution.py:236
  7.2 0.7 copy-start.3
  8.0 0.7 copy-start.4
  8.7 0.7 copy-start.5
  48.1 105.8 %reduce-scatter.2.cloned.1.call-start = ((), (), s32[]{:S(2)}) async-start(), calls=%async_computation.5 | async-start | bytes 2359296 | tf_op jit(solution)/shard_map/reduce_scatter | solution.py:314
  56.0 1.9 copy-start.6
  98.3 6.2 %collective-permute-start = (bf16[8,512,256]{2,1,0:T(8,128)(2,1)S(1)}, bf16[8,512,256]{2,1,0:T(8,128)(2,1)S(1)}, u32[]{:S(2)}, u32[]{:S(2)}) collective-permute-start(bf16[8,512,256]{2,1,0:T(8,128)(2,1)S(1)} %get-tuple-element.30), channel_id=1, source_target_pairs={{0,1},{1,0},{2,3},{3,2},{4,5},{5,4},{6,7},{7,6},{8,9},{9,8},{10,11... | collective-permute-start | bytes 6291464 | tf_op jit(solution)/shard_map/ppermute | solution.py:291
  106.4 11.0 %copy-start = (bf16[64,8,256]{2,1,0:T(8,128)(2,1)S(1)}, bf16[64,8,256]{2,1,0:T(8,128)(2,1)}, u32[]{:S(2)}) copy-start(bf16[64,8,256]{2,1,0:T(8,128)(2,1)} %all_to_all.20) | copy-start | bytes 786436
  106.4 47.5 %copy-start.2 = (bf16[128,128]{1,0:T(8,128)(2,1)S(1)}, bf16[128,128]{1,0:T(8,128)(2,1)}, u32[]{:S(2)}) copy-start(bf16[128,128]{1,0:T(8,128)(2,1)} %constant.31.clone.fold_ref) | copy-start | bytes 98308
  107.0 10.3 %all-to-all-start.1 = ((f32[16,1,512]{2,1,0:T(1,128)}), f32[16,1,512]{2,1,0:T(1,128)S(1)}, u32[]{:S(2)}, u32[]{:S(2)}) async-start(f32[16,1,512]{2,1,0:T(1,128)} %broadcast_in_dim.13), calls=%async_computation.2 | async-start | bytes 65536 | tf_op jit(solution)/shard_map/all_to_all | solution.py:318
  118.7 25.9 %all-to-all-start.2 = ((f32[64,1,128]{2,1,0:T(1,128)}), f32[64,1,128]{2,1,0:T(1,128)S(1)}, u32[]{:S(2)}, u32[]{:S(2)}) async-start(f32[64,1,128]{2,1,0:T(1,128)} %bitcast.17), calls=%async_computation.3 | async-start | bytes 65536 | tf_op jit(solution)/shard_map/all_to_all | solution.py:333
  153.9 1.0 copy-start.1
Sparse Core Ops, SparseCore 0:
  48.2 38.4 all-gather.2
  106.5 47.3 reduce-scatter.1

commit v3 on v2

--- a/solution.py
+++ b/solution.py
@@ -11,7 +11,7 @@
 F32 = jnp.float32
 BF16 = jnp.bfloat16
 LANES = 128
-VMEM_LIMIT = 48 * 1024 * 1024
+VMEM_LIMIT = 24 * 1024 * 1024
 VMEM = pl.BlockSpec(memory_space=pltpu.VMEM)
 SMEM = pl.BlockSpec(memory_space=pltpu.SMEM)
 
@@ -57,23 +57,26 @@
         slots_ref[:, at + width : at + LANES] = blank
 
 
-def terms(pre, hidden, gating, front_ref, back_ref, which, out_ref):
-    pairs = out_ref.shape[0]
-    offsets = [pl.multiple_of((2 * j + which) * LANES, LANES) for j in range(pairs)]
-    front = jnp.concatenate([front_ref[pl.ds(at, LANES), :] for at in offsets], axis=0)
-    back = jnp.concatenate([back_ref[:, pl.ds(at, LANES)] for at in offsets], axis=1)
-    grad = dot(pre, front, ((1,), (1,)))
-    out = dot(hidden, back)
-    for j in range(pairs):
-        lanes = slice(j * LANES, (j + 1) * LANES)
-        out_ref[j, :, :LANES] = grad[:, lanes].astype(BF16)
-        out_ref[j, :, LANES:] = (gating * out[:, lanes]).astype(BF16)
+def terms(at, pre_ref, hidden_ref, gating_ref, front_ref, back_ref, out_ref):
+    chips = out_ref.shape[0]
+    for pair in range(chips // 2):
+        offsets = [
+            pl.multiple_of((2 * (2 * pair + j) + at) * LANES, LANES) for j in range(2)
+        ]
+        front = jnp.concatenate([front_ref[pl.ds(o, LANES), :] for o in offsets], axis=0)
+        back = jnp.concatenate([back_ref[:, pl.ds(o, LANES)] for o in offsets], axis=1)
+        grad = dot(pre_ref[...], front, ((1,), (1,)))
+        out = dot(hidden_ref[...], back)
+        for j in range(2):
+            lanes = slice(j * LANES, (j + 1) * LANES)
+            out_ref[2 * pair + j, :, :LANES] = grad[:, lanes].astype(BF16)
+            out_ref[2 * pair + j, :, LANES:] = (gating_ref[...] * out[:, lanes]).astype(BF16)
 
 
 def expert_kernel(
     experts,
     at_ref,
-    got_ref,
+    whole_ref,
     front_ref,
     back_ref,
     router_ref,
@@ -83,73 +86,74 @@
     gating_ref,
     gate_ref,
     chance_ref,
+    got,
     acc,
     proj,
     rates,
+    sems,
 ):
-    phase, step = pl.program_id(0), pl.program_id(1)
-    per_step, slots = got_ref.shape[0], got_ref.shape[1]
-
-    @pl.when(phase == 0)
-    def _():
-        tok = jnp.concatenate([got_ref[j, :, :LANES] for j in range(per_step)], axis=1)
-        cot = jnp.concatenate([got_ref[j, :, LANES:] for j in range(per_step)], axis=1)
-
-        @pl.when(step == 0)
-        def _():
-            acc[...] = dot(tok, front_ref[...])
-            proj[...] = dot(cot, back_ref[...], ((1,), (1,)))
-            rates[...] = dot(tok, router_ref[...], ((1,), (1,)))
-
-        @pl.when(step > 0)
-        def _():
-            acc[...] += dot(tok, front_ref[...])
-            proj[...] += dot(cot, back_ref[...], ((1,), (1,)))
-            rates[...] += dot(tok, router_ref[...], ((1,), (1,)))
-
-    @pl.when((phase == 0) & (step == pl.num_programs(1) - 1))
-    def _():
-        chunk = 64
-        own = at_ref[0]
-
-        def one(i, carry):
-            rows = pl.ds(pl.multiple_of(i * chunk, chunk), chunk)
-            scores = rates[rows, :]
-            lane = lax.broadcasted_iota(jnp.int32, scores.shape, 1)
-            scores = jnp.where(lane < experts, scores, -jnp.inf)
-            top = jnp.max(scores, axis=1, keepdims=True)
-            raised = jnp.exp(scores - top)
-            chances = raised / jnp.sum(raised, axis=1, keepdims=True)
-            gating = jnp.sum(jnp.where(lane == own, chances, 0.0), axis=1, keepdims=True)
-            x = acc[rows, :]
-            up = proj[rows, :]
-            c = np.float32(np.sqrt(2.0 / np.pi))
-            square = x * x
-            t = jnp.tanh(c * (x + 0.044715 * (square * x)))
-            half = 0.5 * (1.0 + t)
-            hidden = (x * half).astype(BF16)
-            slope = half + 0.5 * x * (1.0 - t * t) * (c * (1.0 + 3 * 0.044715 * square))
-            pre_ref[rows, :] = (slope * (gating * up)).astype(BF16)
-            hidden_ref[rows, :] = hidden
-            gate = jnp.sum(hidden.astype(F32) * up, axis=1, keepdims=True)
-            rates[rows, :] = jnp.where(lane == experts, gate, chances)
-            gating_ref[rows, :] = jnp.broadcast_to(gating, (chunk, LANES))
-            return carry
-
-        lax.fori_loop(0, slots // chunk, one, 0)
-        turned = rates[...].T
-        chance_ref[...] = turned[:experts]
-        gate_ref[...] = turned[experts : experts + 8]
-
-    @pl.when(phase == 1)
-    def _():
-        terms(
-            pre_ref[...], hidden_ref[...], gating_ref[...], front_ref, back_ref, 1 - at_ref[1], send_ref
+    parts = sems.shape[0]
+    per_part = got.shape[0] // parts
+    slots = got.shape[1]
+    depth = per_part * LANES
+    copies = [
+        pltpu.make_async_copy(
+            whole_ref.at[pl.ds(i * per_part, per_part)], got.at[pl.ds(i * per_part, per_part)], sems.at[i]
         )
+        for i in range(parts)
+    ]
+    for copy in copies:
+        copy.start()
+    for i in range(parts):
+        copies[i].wait()
+        blocks = range(i * per_part, (i + 1) * per_part)
+        tok = jnp.concatenate([got[j, :, :LANES] for j in blocks], axis=1)
+        cot = jnp.concatenate([got[j, :, LANES:] for j in blocks], axis=1)
+        span = slice(i * depth, (i + 1) * depth)
+        new = (
+            dot(tok, front_ref[span, :]),
+            dot(cot, back_ref[:, span], ((1,), (1,))),
+            dot(tok, router_ref[:, span], ((1,), (1,))),
+        )
+        for ref, value in zip((acc, proj, rates), new):
+            ref[...] = value if i == 0 else ref[...] + value
+
+    chunk = min(128, slots)
+    own = at_ref[0]
+
+    def one(i, carry):
+        rows = pl.ds(pl.multiple_of(i * chunk, chunk), chunk)
+        scores = rates[rows, :]
+        lane = lax.broadcasted_iota(jnp.int32, scores.shape, 1)
+        scores = jnp.where(lane < experts, scores, -jnp.inf)
+        top = jnp.max(scores, axis=1, keepdims=True)
+        raised = jnp.exp(scores - top)
+        chances = raised / jnp.sum(raised, axis=1, keepdims=True)
+        gating = jnp.sum(jnp.where(lane == own, chances, 0.0), axis=1, keepdims=True)
+        x = acc[rows, :]
+        up = proj[rows, :]
+        c = np.float32(np.sqrt(2.0 / np.pi))
+        square = x * x
+        t = jnp.tanh(c * (x + 0.044715 * (square * x)))
+        half = 0.5 * (1.0 + t)
+        hidden = (x * half).astype(BF16)
+        slope = half + 0.5 * x * (1.0 - t * t) * (c * (1.0 + 3 * 0.044715 * square))
+        pre_ref[rows, :] = (slope * (gating * up)).astype(BF16)
+        hidden_ref[rows, :] = hidden
+        gate = jnp.sum(hidden.astype(F32) * up, axis=1, keepdims=True)
+        rates[rows, :] = jnp.where(lane == experts, gate, chances)
+        gating_ref[rows, :] = jnp.broadcast_to(gating, (chunk, LANES))
+        return carry
+
+    lax.fori_loop(0, slots // chunk, one, 0)
+    turned = rates[...].T
+    chance_ref[...] = turned[:experts]
+    gate_ref[...] = turned[experts : experts + 8]
+    terms(1 - at_ref[1], pre_ref, hidden_ref, gating_ref, front_ref, back_ref, send_ref)
 
 
 def keep_kernel(at_ref, pre_ref, hidden_ref, gating_ref, front_ref, back_ref, keep_ref):
-    terms(pre_ref[...], hidden_ref[...], gating_ref[...], front_ref, back_ref, at_ref[1], keep_ref)
+    terms(at_ref[1], pre_ref, hidden_ref, gating_ref, front_ref, back_ref, keep_ref)
 
 
 def router_kernel(at_ref, gates_ref, chance_ref, slots_ref, score_ref, part_ref):
@@ -220,13 +224,27 @@
         fold[lane, width + lane % per_row] = 1
     fold = jnp.asarray(fold, BF16)
 
-    mine, pick = call(
+    whole_block = lambda i: (0, 0)
+    mine, pick = pl.pallas_call(
         functools.partial(place_kernel, capacity, experts),
-        (
+        grid=(1,),
+        in_specs=[
+            pl.BlockSpec((2, tok_count), whole_block),
+            pl.BlockSpec((width, tok_count), whole_block),
+            pl.BlockSpec((width, tok_count), whole_block),
+        ],
+        out_specs=[
+            pl.BlockSpec((slots, lanes), whole_block),
+            pl.BlockSpec((slots, tok_count), whole_block),
+        ],
+        out_shape=(
             jax.ShapeDtypeStruct((slots, lanes), BF16),
             jax.ShapeDtypeStruct((slots, tok_count), BF16),
         ),
-        [VMEM] * 3,
+        compiler_params=pltpu.CompilerParams(vmem_limit_bytes=60 * 1024 * 1024),
+        cost_estimate=pl.CostEstimate(
+            flops=60_000_000, bytes_accessed=500_000, transcendentals=0
+        ),
     )(routes.T, tokens.T, cotangent.T)
     got = lax.all_to_all(
         mine.reshape(sources, capacity, lanes), "expert", split_axis=0, concat_axis=0, tiled=True
@@ -244,36 +262,17 @@
         router.T.reshape(experts, groups, width), ((0, LANES - experts), (0, 0), (0, spare))
     ).reshape(LANES, groups * LANES)
 
-    per_step = 4
-    steps = groups // per_step
-    depth = per_step * LANES
     send, pre, hidden, gating, gate_term, chances = pl.pallas_call(
         functools.partial(expert_kernel, experts),
-        grid_spec=pltpu.PrefetchScalarGridSpec(
-            num_scalar_prefetch=1,
-            grid=(2, steps),
-            in_specs=[
-                pl.BlockSpec(
-                    (per_step, slots, lanes), lambda p, i, at: (i * (1 - p) + (steps - 1) * p, 0, 0)
-                ),
-                pl.BlockSpec((depth, ff), lambda p, i, at: (i, 0)),
-                pl.BlockSpec((ff, depth), lambda p, i, at: (0, i)),
-                pl.BlockSpec((LANES, depth), lambda p, i, at: (0, i * (1 - p) + (steps - 1) * p)),
-            ],
-            out_specs=[
-                pl.BlockSpec((per_step // 2, slots, lanes), lambda p, i, at: (i * p, 0, 0)),
-                pl.BlockSpec((slots, ff), lambda p, i, at: (0, 0)),
-                pl.BlockSpec((slots, ff), lambda p, i, at: (0, 0)),
-                pl.BlockSpec((slots, LANES), lambda p, i, at: (0, 0)),
-                pl.BlockSpec((8, slots), lambda p, i, at: (0, 0)),
-                pl.BlockSpec((experts, slots), lambda p, i, at: (0, 0)),
-            ],
-            scratch_shapes=[
-                pltpu.VMEM((slots, ff), F32),
-                pltpu.VMEM((slots, ff), F32),
-                pltpu.VMEM((slots, LANES), F32),
-            ],
-        ),
+        in_specs=[SMEM, pl.BlockSpec(memory_space=pltpu.HBM), VMEM, VMEM, VMEM],
+        out_specs=[VMEM] * 6,
+        scratch_shapes=[
+            pltpu.VMEM((groups, slots, lanes), BF16),
+            pltpu.VMEM((slots, ff), F32),
+            pltpu.VMEM((slots, ff), F32),
+            pltpu.VMEM((slots, LANES), F32),
+            pltpu.SemaphoreType.DMA((4,)),
+        ],
         out_shape=(
             jax.ShapeDtypeStruct((chips, slots, lanes), BF16),
             jax.ShapeDtypeStruct((slots, ff), BF16),
@@ -282,34 +281,21 @@
             jax.ShapeDtypeStruct((8, slots), F32),
             jax.ShapeDtypeStruct((experts, slots), F32),
         ),
-        compiler_params=pltpu.CompilerParams(vmem_limit_bytes=VMEM_LIMIT),
+        compiler_params=pltpu.CompilerParams(vmem_limit_bytes=44 * 1024 * 1024),
         cost_estimate=pl.CostEstimate(
             flops=4_000_000_000, bytes_accessed=16_000_000, transcendentals=slots * ff
         ),
     )(at, whole, front, back, scorer)
 
     swapped = lax.ppermute(send, "dp", swap)
-    keep = pl.pallas_call(
+    keep = call(
         keep_kernel,
-        grid_spec=pltpu.PrefetchScalarGridSpec(
-            num_scalar_prefetch=1,
-            grid=(steps,),
-            in_specs=[
-                pl.BlockSpec((slots, ff), lambda i, at: (0, 0)),
-                pl.BlockSpec((slots, ff), lambda i, at: (0, 0)),
-                pl.BlockSpec((slots, LANES), lambda i, at: (0, 0)),
-                pl.BlockSpec((depth, ff), lambda i, at: (i, 0)),
-                pl.BlockSpec((ff, depth), lambda i, at: (0, i)),
-            ],
-            out_specs=pl.BlockSpec((per_step // 2, slots, lanes), lambda i, at: (i, 0, 0)),
-        ),
-        out_shape=jax.ShapeDtypeStruct((chips, slots, lanes), BF16),
-        compiler_params=pltpu.CompilerParams(vmem_limit_bytes=VMEM_LIMIT),
-        cost_estimate=pl.CostEstimate(
-            flops=2_000_000_000, bytes_accessed=8_000_000, transcendentals=0
-        ),
+        jax.ShapeDtypeStruct((chips, slots, lanes), BF16),
+        [SMEM] + [VMEM] * 5,
+        flops=2_000_000_000,
+        moved=8_000_000,
     )(at, pre, hidden, gating, front, back)
-    halves = (keep.astype(F32) + swapped.astype(F32)).astype(BF16)
+    halves = keep + swapped
     halves, gate_term = lax.optimization_barrier((halves, gate_term))
     sums = lax.psum_scatter(
         halves, "dp", scatter_dimension=0, axis_index_groups=same_core, tiled=True

time: 191 us -> 189 us (0.990)
  Pallas kernels: 18.6 us -> 14.8 us
    pallas_call x3, Pallas kernels: 16 us -> 12.1 us  [the longest x1 8.41 us: shards(): pl.pallas_call(functools.partial(expert_kernel, experts), in_specs=[SMEM,...]
    ppermute x1, waiting for transfers between devices: 0.01 us -> 2.05 us  [shards(): swapped = lax.ppermute(send, 'dp', swap)]
  transfers between devices with their start and end apart: 5 -> 5, of which waited for: 4 -> 5; matrix products, arithmetic and copies ran while one was open for 6% -> 6% of each run, Pallas kernels for 3% -> 2%
where the time goes in v3:
time: 189 us; the launch traced here: 188 us
  blocking collectives  65.9 us (35%)
  waiting for transfers between devices  54.9 us (29%)
  starting transfers between devices  21.8 us (12%)
  Pallas kernels  14.8 us (8%)
  local copies, waits for them, and re-layouts  14.5 us (8%)
  between operations  14.2 us (8%)
  other arithmetic  1.91 us (1%)
    all_to_all x1, blocking collectives, shards(): lax.all_to_all(mine.reshape(sources, capacity, lanes), 'expert', split_ax...  38.5 us
    all_to_all x1, blocking collectives, shards(): lax.all_to_all(home.reshape(sources, capacity, lanes), 'expert', split_ax...  27.4 us
    all_gather x1, waiting for transfers between devices, shards(): whole = lax.all_gather(got[None], 'dp', axis=0, tiled=True)  27.2 us
    all_to_all x1, starting transfers between devices, shards(): lax.all_to_all(router_part.reshape(experts, 1, LANES), 'expert', split_ax...  14 us
    all_to_all x1, waiting for transfers between devices, shards(): lax.all_to_all(router_part.reshape(experts, 1, LANES), 'expert', split_ax...  11.8 us
    reduce_scatter x1, waiting for transfers between devices, shards(): lax.psum_scatter(halves, 'dp', scatter_dimension=0, axis_index_groups=sam...  9.21 us
    pallas_call x1, Pallas kernels, shards(): pl.pallas_call(functools.partial(expert_kernel, experts), in_specs=[SMEM,...  8.41 us
    all_to_all x1, starting transfers between devices, shards(): lax.all_to_all(jnp.broadcast_to(gate_term[None, :1], (groups, 1, slots)),...  5.65 us
  transfers between devices with their start and end apart: 5, of which 5 were waited for; matrix products, arithmetic and copies ran while one was open for 6% of the time, Pallas kernels for 2%

profile of v3, /device:TPU:6, one launch (start us, length us, event | category | flops | bytes accessed | tf_op | source)
XLA Modules:
  0.0 188.0 jit_solution(6716572875733005148)
XLA Ops:
  7.2 0.0 all-gather.3.cloned.1.call-start
  7.2 1.8 shard_map.94
  9.1 38.5 %all_to_all.20 = bf16[64,8,256]{2,1,0:T(8,128)(2,1)} all-to-all(bf16[64,8,256]{2,1,0:T(8,128)(2,1)} %bitcast.47), channel_id=1, replica_groups=mesh['expert'=64,'dp'=16] {'expert'}, dimensions={0} | all-to-all | bytes 524288 | tf_op jit(solution)/shard_map/all_to_all | solution.py:249
  47.6 0.0 all-gather.3.cloned.1.call-update
  47.6 0.0 reduce-scatter.2.cloned.1.call-start
  47.6 0.1 pad_add_fusion.at_ref
  47.7 2.8 %copy.12 = bf16[1,512,1664]{1,2,0:T(8,128)(2,1)S(1)} copy(bf16[1,512,1664]{2,1,0:T(8,128)(2,1)} %param.12) | data formatting | bytes 3407872 | tf_op jit(solution)/shard_map/optimization_barrier | solution.py:253
  50.6 1.6 pad.17
  52.1 2.9 %copy.15.back_ref = bf16[512,2048]{1,0:T(8,128)(2,1)S(1)} copy(bf16[512,2048]{0,1:T(8,128)(2,1)} %bitcast.43) | data formatting | bytes 4194304 | tf_op jit(solution)/shard_map/reshape | solution.py:260
  55.1 0.0 copy-start.5
  55.1 3.2 %pad.16 = bf16[16,128,512]{2,1,0:T(8,128)(2,1)} pad(bf16[16,104,512]{2,1,0:T(8,128)(2,1)} %bitcast.46, bf16[]{:T(256)} %constant.28.clone.1), padding=0_0x0_24x0_0 | pad | bytes 3801090 | tf_op jit(solution)/shard_map/jit(_pad)/pad | solution.py:257
  58.3 0.0 copy-done.5
  58.3 0.5 reshape.49
  58.8 0.1 pad.18
  58.9 0.1 copy.20
  59.0 27.2 %all-gather.3.cloned.1.call-done = bf16[8192,256]{1,0:T(8,128)(2,1)} async-done(((bf16[512,256]{1,0:T(8,128)(2,1)}), bf16[8192,256]{1,0:T(8,128)(2,1)}) %all-gather.3.cloned.1.call-update) | async-done | bytes 4194320 | tf_op jit(solution)/shard_map/all_gather | solution.py:254
  86.2 0.0 copy-start
  86.2 1.6 copy-done
  87.8 8.4 %shard_map.95 = (bf16[8,512,256]{2,1,0:T(8,128)(2,1)S(1)}, bf16[512,512]{1,0:T(8,128)(2,1)S(1)}, bf16[512,512]{1,0:T(8,128)(2,1)S(1)}, f32[512,128]{1,0:T(8,128)...) custom-call(s32[2]{0:T(128)S(1)} %pad_add_fusion.at_ref, bf16[16,512,256]{2,1,0:T(8,128)(2,1)} %bitcast.50, ...), custom_call_target="tpu_custom_call" | custom-call | flops 4000000000 | bytes 16000000 | tf_op jit(solution)/shard_map/pallas_call | solution.py:265
  96.2 2.1 %collective-permute-start = (bf16[8,512,256]{2,1,0:T(8,128)(2,1)S(1)}, bf16[8,512,256]{2,1,0:T(8,128)(2,1)S(1)}, u32[]{:S(2)}, u32[]{:S(2)}) collective-permute-start(bf16[8,512,256]{2,1,0:T(8,128)(2,1)S(1)} %get-tuple-element.30), channel_id=1, source_target_pairs={{0,1},{1,0},{2,3},{3,2},{4,5},{5,4},{6,7},{7,6},{8,9},{9,8},{10,11... | collective-permute-start | bytes 6291464 | tf_op jit(solution)/shard_map/ppermute | solution.py:290
  98.4 1.9 shard_map.96
  100.3 2.0 %collective-permute-done = bf16[8,512,256]{2,1,0:T(8,128)(2,1)S(1)} collective-permute-done((bf16[8,512,256]{2,1,0:T(8,128)(2,1)S(1)}, bf16[8,512,256]{2,1,0:T(8,128)(2,1)S(1)}, u32[]{:S(2)}, u32[]{:S(2)}) %collective-permute-start) | collective-permute-done | bytes 2097184 | tf_op jit(solution)/shard_map/ppermute | solution.py:290
  102.3 1.8 add.21
  104.1 0.0 copy-start.1
  104.1 0.0 copy-start.4
  104.1 0.0 copy-start.3
  104.1 0.0 reduce-scatter.2.cloned.1.call-update
  104.2 0.6 broadcast_in_dim.13
  104.8 5.7 %all-to-all-start.1 = ((f32[16,1,512]{2,1,0:T(1,128)}), f32[16,1,512]{2,1,0:T(1,128)S(1)}, u32[]{:S(2)}, u32[]{:S(2)}) async-start(f32[16,1,512]{2,1,0:T(1,128)} %broadcast_in_dim.13), calls=%async_computation.2 | async-start | bytes 65536 | tf_op jit(solution)/shard_map/all_to_all | solution.py:304
  110.5 4.6 %all-to-all-done.1 = f32[16,1,512]{2,1,0:T(1,128)S(1)} async-done(((f32[16,1,512]{2,1,0:T(1,128)}), f32[16,1,512]{2,1,0:T(1,128)S(1)}, u32[]{:S(2)}, u32[]{:S(2)}) %all-to-all-start.1) | async-done | bytes 32800 | tf_op jit(solution)/shard_map/all_to_all | solution.py:304
  115.1 0.0 copy-done.1
  115.1 1.3 shard_map.97
  116.4 14.0 %all-to-all-start.2 = ((f32[64,1,128]{2,1,0:T(1,128)}), f32[64,1,128]{2,1,0:T(1,128)S(1)}, u32[]{:S(2)}, u32[]{:S(2)}) async-start(f32[64,1,128]{2,1,0:T(1,128)} %bitcast.17), calls=%async_computation.3 | async-start | bytes 65536 | tf_op jit(solution)/shard_map/all_to_all | solution.py:319
  130.4 0.1 dynamic-slice_bitcast_fusion
  130.5 11.8 %all-to-all-done.2 = f32[64,1,128]{2,1,0:T(1,128)S(1)} async-done(((f32[64,1,128]{2,1,0:T(1,128)}), f32[64,1,128]{2,1,0:T(1,128)S(1)}, u32[]{:S(2)}, u32[]{:S(2)}) %all-to-all-start.2) | async-done | bytes 32800 | tf_op jit(solution)/shard_map/all_to_all | solution.py:319
  142.3 9.2 %reduce-scatter.2.cloned.1.call-done = bf16[1,512,256]{2,1,0:T(8,128)(2,1)} async-done(((bf16[8,512,256]{2,1,0:T(8,128)(2,1)}), bf16[1,512,256]{2,1,0:T(8,128)(2,1)}) %reduce-scatter.2.cloned.1.call-update) | async-done | bytes 262160 | tf_op jit(solution)/shard_map/reduce_scatter | solution.py:300
  151.5 0.0 copy-done.4
  151.5 0.0 copy-start.2
  151.5 0.9 copy-done.2
  152.5 0.3 shard_map.98
  152.8 27.4 %all_to_all.21 = bf16[64,8,256]{2,1,0:T(8,128)(2,1)S(1)} all-to-all(bf16[64,8,256]{2,1,0:T(8,128)(2,1)S(1)} %bitcast.38), channel_id=1, replica_groups=mesh['expert'=64,'dp'=16] {'expert'}, dimensions={0} | all-to-all | bytes 524288 | tf_op jit(solution)/shard_map/all_to_all | solution.py:330
  180.1 0.0 copy-done.3
  180.1 1.0 shard_map.99
  (3 shorter events, 0.0 us)
Async XLA Ops:
  7.2 79.1 %all-gather.3.cloned.1.call-start = ((), (), s32[]{:S(2)}) async-start(), calls=%async_computation.6 | async-start | bytes 4456448 | tf_op jit(solution)/shard_map/all_gather | solution.py:254
  47.6 103.9 %reduce-scatter.2.cloned.1.call-start = ((), (), s32[]{:S(2)}) async-start(), calls=%async_computation.5 | async-start | bytes 2359296 | tf_op jit(solution)/shard_map/reduce_scatter | solution.py:300
  55.1 3.2 %copy-start.5 = (bf16[1664,64]{0,1:T(8,128)(2,1)S(1)}, bf16[1664,64]{0,1:T(8,128)(2,1)}, u32[]{:S(2)}) copy-start(bf16[1664,64]{0,1:T(8,128)(2,1)} %param.10) | copy-start | bytes 638980
  86.2 1.6 copy-start
  96.2 6.1 %collective-permute-start = (bf16[8,512,256]{2,1,0:T(8,128)(2,1)S(1)}, bf16[8,512,256]{2,1,0:T(8,128)(2,1)S(1)}, u32[]{:S(2)}, u32[]{:S(2)}) collective-permute-start(bf16[8,512,256]{2,1,0:T(8,128)(2,1)S(1)} %get-tuple-element.30), channel_id=1, source_target_pairs={{0,1},{1,0},{2,3},{3,2},{4,5},{5,4},{6,7},{7,6},{8,9},{9,8},{10,11... | collective-permute-start | bytes 6291464 | tf_op jit(solution)/shard_map/ppermute | solution.py:290
  104.1 11.0 %copy-start.1 = (bf16[64,8,256]{2,1,0:T(8,128)(2,1)S(1)}, bf16[64,8,256]{2,1,0:T(8,128)(2,1)}, u32[]{:S(2)}) copy-start(bf16[64,8,256]{2,1,0:T(8,128)(2,1)} %all_to_all.20) | copy-start | bytes 786436
  104.1 47.4 %copy-start.4 = (bf16[128,128]{1,0:T(8,128)(2,1)S(1)}, bf16[128,128]{1,0:T(8,128)(2,1)}, u32[]{:S(2)}) copy-start(bf16[128,128]{1,0:T(8,128)(2,1)} %constant.31.clone.fold_ref) | copy-start | bytes 98308
  104.1 76.0 %copy-start.3 = (bf16[512,128]{1,0:T(8,128)(2,1)S(1)}, bf16[512,128]{1,0:T(8,128)(2,1)}, u32[]{:S(2)}) copy-start(bf16[512,128]{1,0:T(8,128)(2,1)} %get-tuple-element.37.pick_ref) | copy-start | bytes 393220
  104.8 10.3 %all-to-all-start.1 = ((f32[16,1,512]{2,1,0:T(1,128)}), f32[16,1,512]{2,1,0:T(1,128)S(1)}, u32[]{:S(2)}, u32[]{:S(2)}) async-start(f32[16,1,512]{2,1,0:T(1,128)} %broadcast_in_dim.13), calls=%async_computation.2 | async-start | bytes 65536 | tf_op jit(solution)/shard_map/all_to_all | solution.py:304
  116.4 25.9 %all-to-all-start.2 = ((f32[64,1,128]{2,1,0:T(1,128)}), f32[64,1,128]{2,1,0:T(1,128)S(1)}, u32[]{:S(2)}, u32[]{:S(2)}) async-start(f32[64,1,128]{2,1,0:T(1,128)} %bitcast.17), calls=%async_computation.3 | async-start | bytes 65536 | tf_op jit(solution)/shard_map/all_to_all | solution.py:319
  151.5 1.0 copy-start.2
Sparse Core Ops, SparseCore 0:
  47.7 38.4 all-gather.2
  104.3 47.1 reduce-scatter.1

commit v4 on v3

--- a/solution.py
+++ b/solution.py
@@ -13,6 +13,7 @@
 LANES = 128
 VMEM_LIMIT = 24 * 1024 * 1024
 VMEM = pl.BlockSpec(memory_space=pltpu.VMEM)
+HBM = pl.BlockSpec(memory_space=pltpu.HBM)
 SMEM = pl.BlockSpec(memory_space=pltpu.SMEM)
 
 
@@ -57,7 +58,7 @@
         slots_ref[:, at + width : at + LANES] = blank
 
 
-def terms(at, pre_ref, hidden_ref, gating_ref, front_ref, back_ref, out_ref):
+def terms(at, rows, pre, hidden, gating, front_ref, back_ref, out_ref):
     chips = out_ref.shape[0]
     for pair in range(chips // 2):
         offsets = [
@@ -65,12 +66,12 @@
         ]
         front = jnp.concatenate([front_ref[pl.ds(o, LANES), :] for o in offsets], axis=0)
         back = jnp.concatenate([back_ref[:, pl.ds(o, LANES)] for o in offsets], axis=1)
-        grad = dot(pre_ref[...], front, ((1,), (1,)))
-        out = dot(hidden_ref[...], back)
+        grad = dot(pre, front, ((1,), (1,)))
+        out = dot(hidden, back)
         for j in range(2):
             lanes = slice(j * LANES, (j + 1) * LANES)
-            out_ref[2 * pair + j, :, :LANES] = grad[:, lanes].astype(BF16)
-            out_ref[2 * pair + j, :, LANES:] = (gating_ref[...] * out[:, lanes]).astype(BF16)
+            out_ref[2 * pair + j, rows, :LANES] = grad[:, lanes].astype(BF16)
+            out_ref[2 * pair + j, rows, LANES:] = (gating * out[:, lanes]).astype(BF16)
 
 
 def expert_kernel(
@@ -87,51 +88,38 @@
     gate_ref,
     chance_ref,
     got,
-    acc,
-    proj,
-    rates,
+    wide,
     sems,
 ):
-    parts = sems.shape[0]
-    per_part = got.shape[0] // parts
-    slots = got.shape[1]
-    depth = per_part * LANES
-    copies = [
-        pltpu.make_async_copy(
-            whole_ref.at[pl.ds(i * per_part, per_part)], got.at[pl.ds(i * per_part, per_part)], sems.at[i]
-        )
-        for i in range(parts)
-    ]
-    for copy in copies:
+    parts = sems.shape[0] - 1
+    groups, slots = got.shape[0], got.shape[1]
+    chunk = slots // parts
+    own = at_ref[0]
+    copies = []
+    for i in range(parts):
+        rows = pl.ds(i * chunk, chunk)
+        copies.append(pltpu.make_async_copy(whole_ref.at[:, rows], got.at[:, rows], sems.at[i]))
+    wide_copy = pltpu.make_async_copy(back_ref, wide, sems.at[parts])
+    copies[0].start()
+    wide_copy.start()
+    for copy in copies[1:]:
         copy.start()
     for i in range(parts):
         copies[i].wait()
-        blocks = range(i * per_part, (i + 1) * per_part)
-        tok = jnp.concatenate([got[j, :, :LANES] for j in blocks], axis=1)
-        cot = jnp.concatenate([got[j, :, LANES:] for j in blocks], axis=1)
-        span = slice(i * depth, (i + 1) * depth)
-        new = (
-            dot(tok, front_ref[span, :]),
-            dot(cot, back_ref[:, span], ((1,), (1,))),
-            dot(tok, router_ref[:, span], ((1,), (1,))),
-        )
-        for ref, value in zip((acc, proj, rates), new):
-            ref[...] = value if i == 0 else ref[...] + value
-
-    chunk = min(128, slots)
-    own = at_ref[0]
-
-    def one(i, carry):
-        rows = pl.ds(pl.multiple_of(i * chunk, chunk), chunk)
-        scores = rates[rows, :]
+        rows = slice(i * chunk, (i + 1) * chunk)
+        tok = jnp.concatenate([got[j, rows, :LANES] for j in range(groups)], axis=1)
+        cot = jnp.concatenate([got[j, rows, LANES:] for j in range(groups)], axis=1)
+        x = dot(tok, front_ref[...])
+        scores = dot(tok, router_ref[...], ((1,), (1,)))
+        if i == 0:
+            wide_copy.wait()
+        up = dot(cot, wide[...], ((1,), (1,)))
         lane = lax.broadcasted_iota(jnp.int32, scores.shape, 1)
         scores = jnp.where(lane < experts, scores, -jnp.inf)
         top = jnp.max(scores, axis=1, keepdims=True)
         raised = jnp.exp(scores - top)
         chances = raised / jnp.sum(raised, axis=1, keepdims=True)
         gating = jnp.sum(jnp.where(lane == own, chances, 0.0), axis=1, keepdims=True)
-        x = acc[rows, :]
-        up = proj[rows, :]
         c = np.float32(np.sqrt(2.0 / np.pi))
         square = x * x
         t = jnp.tanh(c * (x + 0.044715 * (square * x)))
@@ -141,19 +129,33 @@
         pre_ref[rows, :] = (slope * (gating * up)).astype(BF16)
         hidden_ref[rows, :] = hidden
         gate = jnp.sum(hidden.astype(F32) * up, axis=1, keepdims=True)
-        rates[rows, :] = jnp.where(lane == experts, gate, chances)
         gating_ref[rows, :] = jnp.broadcast_to(gating, (chunk, LANES))
-        return carry
-
-    lax.fori_loop(0, slots // chunk, one, 0)
-    turned = rates[...].T
-    chance_ref[...] = turned[:experts]
-    gate_ref[...] = turned[experts : experts + 8]
-    terms(1 - at_ref[1], pre_ref, hidden_ref, gating_ref, front_ref, back_ref, send_ref)
+        turned = jnp.where(lane == experts, gate, chances).T
+        chance_ref[:, rows] = turned[:experts]
+        gate_ref[:, rows] = turned[experts : experts + 8]
+        terms(
+            1 - at_ref[1],
+            rows,
+            pre_ref[rows, :],
+            hidden_ref[rows, :],
+            gating_ref[rows, :],
+            front_ref,
+            wide,
+            send_ref,
+        )
 
 
 def keep_kernel(at_ref, pre_ref, hidden_ref, gating_ref, front_ref, back_ref, keep_ref):
-    terms(at_ref[1], pre_ref, hidden_ref, gating_ref, front_ref, back_ref, keep_ref)
+    terms(
+        at_ref[1],
+        slice(None),
+        pre_ref[...],
+        hidden_ref[...],
+        gating_ref[...],
+        front_ref,
+        back_ref,
+        keep_ref,
+    )
 
 
 def router_kernel(at_ref, gates_ref, chance_ref, slots_ref, score_ref, part_ref):
@@ -264,14 +266,12 @@
 
     send, pre, hidden, gating, gate_term, chances = pl.pallas_call(
         functools.partial(expert_kernel, experts),
-        in_specs=[SMEM, pl.BlockSpec(memory_space=pltpu.HBM), VMEM, VMEM, VMEM],
+        in_specs=[SMEM, HBM, VMEM, HBM, VMEM],
         out_specs=[VMEM] * 6,
         scratch_shapes=[
             pltpu.VMEM((groups, slots, lanes), BF16),
-            pltpu.VMEM((slots, ff), F32),
-            pltpu.VMEM((slots, ff), F32),
-            pltpu.VMEM((slots, LANES), F32),
-            pltpu.SemaphoreType.DMA((4,)),
+            pltpu.VMEM((ff, groups * LANES), BF16),
+            pltpu.SemaphoreType.DMA((3,)),
         ],
         out_shape=(
             jax.ShapeDtypeStruct((chips, slots, lanes), BF16),
@@ -281,7 +281,7 @@
             jax.ShapeDtypeStruct((8, slots), F32),
             jax.ShapeDtypeStruct((experts, slots), F32),
         ),
-        compiler_params=pltpu.CompilerParams(vmem_limit_bytes=44 * 1024 * 1024),
+        compiler_params=pltpu.CompilerParams(vmem_limit_bytes=47 * 1024 * 1024),
         cost_estimate=pl.CostEstimate(
             flops=4_000_000_000, bytes_accessed=16_000_000, transcendentals=slots * ff
         ),

time: 189 us -> 187 us (0.989)
  local copies, waits for them, and re-layouts: 14.5 us -> 12.1 us
where the time goes in v4:
time: 187 us; the launch traced here: 186 us
  blocking collectives  66 us (35%)
  waiting for transfers between devices  55.6 us (30%)
  starting transfers between devices  21.8 us (12%)
  Pallas kernels  14.5 us (8%)
  between operations  14.2 us (8%)
  local copies, waits for them, and re-layouts  12.1 us (6%)
  other arithmetic  1.91 us (1%)
    all_to_all x1, blocking collectives, shards(): lax.all_to_all(mine.reshape(sources, capacity, lanes), 'expert', split_ax...  38.5 us
    all_gather x1, waiting for transfers between devices, shards(): whole = lax.all_gather(got[None], 'dp', axis=0, tiled=True)  28.1 us
    all_to_all x1, blocking collectives, shards(): lax.all_to_all(home.reshape(sources, capacity, lanes), 'expert', split_ax...  27.5 us
    all_to_all x1, starting transfers between devices, shards(): lax.all_to_all(router_part.reshape(experts, 1, LANES), 'expert', split_ax...  14 us
    all_to_all x1, waiting for transfers between devices, shards(): lax.all_to_all(router_part.reshape(experts, 1, LANES), 'expert', split_ax...  11.8 us
    reduce_scatter x1, waiting for transfers between devices, shards(): lax.psum_scatter(halves, 'dp', scatter_dimension=0, axis_index_groups=sam...  9.01 us
    pallas_call x1, Pallas kernels, shards(): pl.pallas_call(functools.partial(expert_kernel, experts), in_specs=[SMEM,...  8.16 us
    all_to_all x1, starting transfers between devices, shards(): lax.all_to_all(jnp.broadcast_to(gate_term[None, :1], (groups, 1, slots)),...  5.65 us
  transfers between devices with their start and end apart: 5, of which 5 were waited for; matrix products, arithmetic and copies ran while one was open for 6% of the time, Pallas kernels for 2%

profile of v4, /device:TPU:6, one launch (start us, length us, event | category | flops | bytes accessed | tf_op | source)
XLA Modules:
  0.0 186.1 jit_solution(10462060116384920211)
XLA Ops:
  7.2 0.0 all-gather.3.cloned.1.call-start
  7.2 1.8 shard_map.94
  9.1 38.5 %all_to_all.20 = bf16[64,8,256]{2,1,0:T(8,128)(2,1)} all-to-all(bf16[64,8,256]{2,1,0:T(8,128)(2,1)} %bitcast.47), channel_id=1, replica_groups=mesh['expert'=64,'dp'=16] {'expert'}, dimensions={0} | all-to-all | bytes 524288 | tf_op jit(solution)/shard_map/all_to_all | solution.py:251
  47.6 0.0 all-gather.3.cloned.1.call-update
  47.6 0.0 reduce-scatter.2.cloned.1.call-start
  47.6 0.1 pad_add_fusion.at_ref
  47.7 3.6 %copy.12 = bf16[1,512,1664]{1,2,0:T(8,128)(2,1)} copy(bf16[1,512,1664]{2,1,0:T(8,128)(2,1)} %param.12) | data formatting | bytes 3407872 | tf_op jit(solution)/shard_map/optimization_barrier | solution.py:255
  51.3 1.7 pad.17
  53.0 2.5 %copy.15.back_ref = bf16[512,2048]{1,0:T(8,128)(2,1)} copy(bf16[512,2048]{0,1:T(8,128)(2,1)S(1)} %bitcast.43) | data formatting | bytes 4194304 | tf_op jit(solution)/shard_map/reshape | solution.py:262
  55.5 0.0 copy-start.5
  55.5 1.9 %pad.16 = bf16[16,128,512]{2,1,0:T(8,128)(2,1)S(1)} pad(bf16[16,104,512]{2,1,0:T(8,128)(2,1)} %bitcast.46, bf16[]{:T(256)} %constant.28.clone.1), padding=0_0x0_24x0_0 | pad | bytes 3801090 | tf_op jit(solution)/shard_map/jit(_pad)/pad | solution.py:259
  57.4 0.0 copy-done.5
  57.4 0.5 reshape.49
  57.9 0.1 pad.18
  58.0 0.1 copy.20
  58.1 28.1 %all-gather.3.cloned.1.call-done = bf16[8192,256]{1,0:T(8,128)(2,1)} async-done(((bf16[512,256]{1,0:T(8,128)(2,1)}), bf16[8192,256]{1,0:T(8,128)(2,1)}) %all-gather.3.cloned.1.call-update) | async-done | bytes 4194320 | tf_op jit(solution)/shard_map/all_gather | solution.py:256
  86.2 0.0 copy-start
  86.2 8.2 %shard_map.95 = (bf16[8,512,256]{2,1,0:T(8,128)(2,1)S(1)}, bf16[512,512]{1,0:T(8,128)(2,1)S(1)}, bf16[512,512]{1,0:T(8,128)(2,1)S(1)}, f32[512,128]{1,0:T(8,128)...) custom-call(s32[2]{0:T(128)S(1)} %pad_add_fusion.at_ref, bf16[16,512,256]{2,1,0:T(8,128)(2,1)} %bitcast.50, ...), custom_call_target="tpu_custom_call" | custom-call | flops 4000000000 | bytes 16000000 | tf_op jit(solution)/shard_map/pallas_call | solution.py:267
  94.4 2.1 %collective-permute-start = (bf16[8,512,256]{2,1,0:T(8,128)(2,1)S(1)}, bf16[8,512,256]{2,1,0:T(8,128)(2,1)S(1)}, u32[]{:S(2)}, u32[]{:S(2)}) collective-permute-start(bf16[8,512,256]{2,1,0:T(8,128)(2,1)S(1)} %get-tuple-element.30), channel_id=1, source_target_pairs={{0,1},{1,0},{2,3},{3,2},{4,5},{5,4},{6,7},{7,6},{8,9},{9,8},{10,11... | collective-permute-start | bytes 6291464 | tf_op jit(solution)/shard_map/ppermute | solution.py:290
  96.5 0.0 copy-done
  96.6 1.9 %shard_map.96 = bf16[8,512,256]{2,1,0:T(8,128)(2,1)S(1)} custom-call(s32[2]{0:T(128)S(1)} %pad_add_fusion.at_ref, bf16[512,512]{1,0:T(8,128)(2,1)S(1)} %get-tuple-element.27.pre_ref, bf16[512,512]{1,0:T(8,128)(2,1)S(1)} %get-tuple-element.28.hidden_ref, f32[512,128]{1,0:T(8,128)S(1)} %get-tuple-element.29.gating_ref, bf16[2048,512]{1,0:T(8,128)(2,1)S(1)} %bitcast.34, ...), custom_call_target="tpu_custom_call" | custom-call | flops 2000000000 | bytes 8000000 | tf_op jit(solution)/shard_map/pallas_call | solution.py:291
  98.5 2.0 %collective-permute-done = bf16[8,512,256]{2,1,0:T(8,128)(2,1)S(1)} collective-permute-done((bf16[8,512,256]{2,1,0:T(8,128)(2,1)S(1)}, bf16[8,512,256]{2,1,0:T(8,128)(2,1)S(1)}, u32[]{:S(2)}, u32[]{:S(2)}) %collective-permute-start) | collective-permute-done | bytes 2097184 | tf_op jit(solution)/shard_map/ppermute | solution.py:290
  100.5 1.8 add.21
  102.3 0.0 copy-start.1
  102.3 0.0 copy-start.4
  102.3 0.0 copy-start.3
  102.3 0.0 reduce-scatter.2.cloned.1.call-update
  102.3 0.6 broadcast_in_dim.13
  103.0 5.7 %all-to-all-start.1 = ((f32[16,1,512]{2,1,0:T(1,128)}), f32[16,1,512]{2,1,0:T(1,128)S(1)}, u32[]{:S(2)}, u32[]{:S(2)}) async-start(f32[16,1,512]{2,1,0:T(1,128)} %broadcast_in_dim.13), calls=%async_computation.2 | async-start | bytes 65536 | tf_op jit(solution)/shard_map/all_to_all | solution.py:304
  108.6 4.6 %all-to-all-done.1 = f32[16,1,512]{2,1,0:T(1,128)S(1)} async-done(((f32[16,1,512]{2,1,0:T(1,128)}), f32[16,1,512]{2,1,0:T(1,128)S(1)}, u32[]{:S(2)}, u32[]{:S(2)}) %all-to-all-start.1) | async-done | bytes 32800 | tf_op jit(solution)/shard_map/all_to_all | solution.py:304
  113.3 0.0 copy-done.1
  113.3 1.3 shard_map.97
  114.6 14.0 %all-to-all-start.2 = ((f32[64,1,128]{2,1,0:T(1,128)}), f32[64,1,128]{2,1,0:T(1,128)S(1)}, u32[]{:S(2)}, u32[]{:S(2)}) async-start(f32[64,1,128]{2,1,0:T(1,128)} %bitcast.17), calls=%async_computation.3 | async-start | bytes 65536 | tf_op jit(solution)/shard_map/all_to_all | solution.py:319
  128.6 0.1 dynamic-slice_bitcast_fusion
  128.7 11.8 %all-to-all-done.2 = f32[64,1,128]{2,1,0:T(1,128)S(1)} async-done(((f32[64,1,128]{2,1,0:T(1,128)}), f32[64,1,128]{2,1,0:T(1,128)S(1)}, u32[]{:S(2)}, u32[]{:S(2)}) %all-to-all-start.2) | async-done | bytes 32800 | tf_op jit(solution)/shard_map/all_to_all | solution.py:319
  140.5 9.0 %reduce-scatter.2.cloned.1.call-done = bf16[1,512,256]{2,1,0:T(8,128)(2,1)} async-done(((bf16[8,512,256]{2,1,0:T(8,128)(2,1)}), bf16[1,512,256]{2,1,0:T(8,128)(2,1)}) %reduce-scatter.2.cloned.1.call-update) | async-done | bytes 262160 | tf_op jit(solution)/shard_map/reduce_scatter | solution.py:300
  149.5 0.0 copy-done.4
  149.5 0.0 copy-start.2
  149.5 0.9 copy-done.2
  150.4 0.3 shard_map.98
  150.7 27.5 %all_to_all.21 = bf16[64,8,256]{2,1,0:T(8,128)(2,1)S(1)} all-to-all(bf16[64,8,256]{2,1,0:T(8,128)(2,1)S(1)} %bitcast.38), channel_id=1, replica_groups=mesh['expert'=64,'dp'=16] {'expert'}, dimensions={0} | all-to-all | bytes 524288 | tf_op jit(solution)/shard_map/all_to_all | solution.py:330
  178.2 0.0 copy-done.3
  178.2 1.0 shard_map.99
  (3 shorter events, 0.0 us)
Async XLA Ops:
  7.2 79.1 %all-gather.3.cloned.1.call-start = ((), (), s32[]{:S(2)}) async-start(), calls=%async_computation.6 | async-start | bytes 4456448 | tf_op jit(solution)/shard_map/all_gather | solution.py:256
  47.6 101.9 %reduce-scatter.2.cloned.1.call-start = ((), (), s32[]{:S(2)}) async-start(), calls=%async_computation.5 | async-start | bytes 2359296 | tf_op jit(solution)/shard_map/reduce_scatter | solution.py:300
  55.5 1.9 %copy-start.5 = (bf16[1664,64]{0,1:T(8,128)(2,1)S(1)}, bf16[1664,64]{0,1:T(8,128)(2,1)}, u32[]{:S(2)}) copy-start(bf16[1664,64]{0,1:T(8,128)(2,1)} %param.10) | copy-start | bytes 638980
  86.2 10.3 %copy-start = (bf16[512,2048]{1,0:T(8,128)(2,1)S(1)}, bf16[512,2048]{1,0:T(8,128)(2,1)}, u32[]{:S(2)}) copy-start(bf16[512,2048]{1,0:T(8,128)(2,1)} %copy.15.back_ref) | copy-start | bytes 6291460
  94.4 6.1 %collective-permute-start = (bf16[8,512,256]{2,1,0:T(8,128)(2,1)S(1)}, bf16[8,512,256]{2,1,0:T(8,128)(2,1)S(1)}, u32[]{:S(2)}, u32[]{:S(2)}) collective-permute-start(bf16[8,512,256]{2,1,0:T(8,128)(2,1)S(1)} %get-tuple-element.30), channel_id=1, source_target_pairs={{0,1},{1,0},{2,3},{3,2},{4,5},{5,4},{6,7},{7,6},{8,9},{9,8},{10,11... | collective-permute-start | bytes 6291464 | tf_op jit(solution)/shard_map/ppermute | solution.py:290
  102.3 11.0 %copy-start.1 = (bf16[64,8,256]{2,1,0:T(8,128)(2,1)S(1)}, bf16[64,8,256]{2,1,0:T(8,128)(2,1)}, u32[]{:S(2)}) copy-start(bf16[64,8,256]{2,1,0:T(8,128)(2,1)} %all_to_all.20) | copy-start | bytes 786436
  102.3 47.2 %copy-start.4 = (bf16[128,128]{1,0:T(8,128)(2,1)S(1)}, bf16[128,128]{1,0:T(8,128)(2,1)}, u32[]{:S(2)}) copy-start(bf16[128,128]{1,0:T(8,128)(2,1)} %constant.31.clone.fold_ref) | copy-start | bytes 98308
  102.3 75.9 %copy-start.3 = (bf16[512,128]{1,0:T(8,128)(2,1)S(1)}, bf16[512,128]{1,0:T(8,128)(2,1)}, u32[]{:S(2)}) copy-start(bf16[512,128]{1,0:T(8,128)(2,1)} %get-tuple-element.37.pick_ref) | copy-start | bytes 393220
  103.0 10.3 %all-to-all-start.1 = ((f32[16,1,512]{2,1,0:T(1,128)}), f32[16,1,512]{2,1,0:T(1,128)S(1)}, u32[]{:S(2)}, u32[]{:S(2)}) async-start(f32[16,1,512]{2,1,0:T(1,128)} %broadcast_in_dim.13), calls=%async_computation.2 | async-start | bytes 65536 | tf_op jit(solution)/shard_map/all_to_all | solution.py:304
  114.6 25.9 %all-to-all-start.2 = ((f32[64,1,128]{2,1,0:T(1,128)}), f32[64,1,128]{2,1,0:T(1,128)S(1)}, u32[]{:S(2)}, u32[]{:S(2)}) async-start(f32[64,1,128]{2,1,0:T(1,128)} %bitcast.17), calls=%async_computation.3 | async-start | bytes 65536 | tf_op jit(solution)/shard_map/all_to_all | solution.py:319
  149.5 1.0 copy-start.2
Sparse Core Ops, SparseCore 0:
  47.7 38.4 all-gather.2
  102.5 46.9 reduce-scatter.1

commit v5 on v4

--- a/solution.py
+++ b/solution.py
@@ -11,6 +11,7 @@
 F32 = jnp.float32
 BF16 = jnp.bfloat16
 LANES = 128
+EXPERT_VMEM = 42 * 1024 * 1024
 VMEM_LIMIT = 24 * 1024 * 1024
 VMEM = pl.BlockSpec(memory_space=pltpu.VMEM)
 HBM = pl.BlockSpec(memory_space=pltpu.HBM)
@@ -58,20 +59,13 @@
         slots_ref[:, at + width : at + LANES] = blank
 
 
-def terms(at, rows, pre, hidden, gating, front_ref, back_ref, out_ref):
-    chips = out_ref.shape[0]
-    for pair in range(chips // 2):
-        offsets = [
-            pl.multiple_of((2 * (2 * pair + j) + at) * LANES, LANES) for j in range(2)
-        ]
-        front = jnp.concatenate([front_ref[pl.ds(o, LANES), :] for o in offsets], axis=0)
-        back = jnp.concatenate([back_ref[:, pl.ds(o, LANES)] for o in offsets], axis=1)
-        grad = dot(pre, front, ((1,), (1,)))
-        out = dot(hidden, back)
-        for j in range(2):
-            lanes = slice(j * LANES, (j + 1) * LANES)
-            out_ref[2 * pair + j, rows, :LANES] = grad[:, lanes].astype(BF16)
-            out_ref[2 * pair + j, rows, LANES:] = (gating * out[:, lanes]).astype(BF16)
+def terms(both_ref, gating_ref, own_ref, pair):
+    rows = slice(pair * 2 * LANES, (pair + 1) * 2 * LANES)
+    grad = dot(both_ref[0], own_ref[0, rows, :], ((1,), (1,)))
+    out = dot(both_ref[1], own_ref[1, rows, :], ((1,), (1,)))
+    for j in range(2):
+        lanes = slice(j * LANES, (j + 1) * LANES)
+        yield j, grad[:, lanes], gating_ref[...] * out[:, lanes]
 
 
 def expert_kernel(
@@ -81,9 +75,7 @@
     front_ref,
     back_ref,
     router_ref,
-    send_ref,
-    pre_ref,
-    hidden_ref,
+    both_ref,
     gating_ref,
     gate_ref,
     chance_ref,
@@ -113,7 +105,7 @@
         scores = dot(tok, router_ref[...], ((1,), (1,)))
         if i == 0:
             wide_copy.wait()
-        up = dot(cot, wide[...], ((1,), (1,)))
+        up = dot(cot, wide[...])
         lane = lax.broadcasted_iota(jnp.int32, scores.shape, 1)
         scores = jnp.where(lane < experts, scores, -jnp.inf)
         top = jnp.max(scores, axis=1, keepdims=True)
@@ -126,36 +118,28 @@
         half = 0.5 * (1.0 + t)
         hidden = (x * half).astype(BF16)
         slope = half + 0.5 * x * (1.0 - t * t) * (c * (1.0 + 3 * 0.044715 * square))
-        pre_ref[rows, :] = (slope * (gating * up)).astype(BF16)
-        hidden_ref[rows, :] = hidden
+        both_ref[0, rows, :] = (slope * (gating * up)).astype(BF16)
+        both_ref[1, rows, :] = hidden
         gate = jnp.sum(hidden.astype(F32) * up, axis=1, keepdims=True)
         gating_ref[rows, :] = jnp.broadcast_to(gating, (chunk, LANES))
         turned = jnp.where(lane == experts, gate, chances).T
         chance_ref[:, rows] = turned[:experts]
         gate_ref[:, rows] = turned[experts : experts + 8]
-        terms(
-            1 - at_ref[1],
-            rows,
-            pre_ref[rows, :],
-            hidden_ref[rows, :],
-            gating_ref[rows, :],
-            front_ref,
-            wide,
-            send_ref,
-        )
-
-
-def keep_kernel(at_ref, pre_ref, hidden_ref, gating_ref, front_ref, back_ref, keep_ref):
-    terms(
-        at_ref[1],
-        slice(None),
-        pre_ref[...],
-        hidden_ref[...],
-        gating_ref[...],
-        front_ref,
-        back_ref,
-        keep_ref,
-    )
+
+
+def keep_kernel(both_ref, gating_ref, own_ref, keep_ref):
+    for pair in range(keep_ref.shape[0] // 2):
+        for j, grad, out in terms(both_ref, gating_ref, own_ref, pair):
+            keep_ref[2 * pair + j, :, :LANES] = grad.astype(BF16)
+            keep_ref[2 * pair + j, :, LANES:] = out.astype(BF16)
+
+
+def other_kernel(both_ref, gating_ref, own_ref, keep_ref, sum_ref):
+    pair = pl.program_id(0)
+    for j, grad, out in terms(both_ref, gating_ref, own_ref, 0):
+        kept = keep_ref[2 * pair + j].astype(F32)
+        sum_ref[j, :, :LANES] = (grad + kept[:, :LANES]).astype(BF16)
+        sum_ref[j, :, LANES:] = (out + kept[:, LANES:]).astype(BF16)
 
 
 def router_kernel(at_ref, gates_ref, chance_ref, slots_ref, score_ref, part_ref):
@@ -220,7 +204,7 @@
     same_core = [[2 * chip + core for chip in range(chips)] for core in range(2)]
     swap = [(index, index ^ 1) for index in range(groups)]
     dp = lax.axis_index("dp")
-    at = jnp.stack([lax.axis_index("expert"), dp % 2]).astype(jnp.int32)
+    at = lax.axis_index("expert").astype(jnp.int32)[None]
     fold = np.zeros((LANES, LANES), np.float32)
     for lane in range(width):
         fold[lane, width + lane % per_row] = 1
@@ -258,44 +242,64 @@
     spare = LANES - width
     front = jnp.pad(w_in[0].reshape(groups, width, ff), ((0, 0), (0, spare), (0, 0)))
     front = front.reshape(groups * LANES, ff)
-    back = jnp.pad(w_out[0].reshape(ff, groups, width), ((0, 0), (0, 0), (0, spare)))
-    back = back.reshape(ff, groups * LANES)
+    back = jnp.pad(w_out[0].T.reshape(groups, width, ff), ((0, 0), (0, spare), (0, 0)))
+    back = back.reshape(groups * LANES, ff)
+    core = dp % 2
+
+    def half(which):
+        picked = [
+            lax.dynamic_index_in_dim(part.reshape(chips, 2, LANES, ff), which, 1, keepdims=False)
+            for part in (front, back)
+        ]
+        return jnp.stack(picked).reshape(2, chips * LANES, ff)
+
+    own = half(core)
+    other = lax.ppermute(half(1 - core), "dp", swap)
     scorer = jnp.pad(
         router.T.reshape(experts, groups, width), ((0, LANES - experts), (0, 0), (0, spare))
     ).reshape(LANES, groups * LANES)
 
-    send, pre, hidden, gating, gate_term, chances = pl.pallas_call(
+    whole, other, own = lax.optimization_barrier((whole, other, own))
+    both, gating, gate_term, chances = pl.pallas_call(
         functools.partial(expert_kernel, experts),
         in_specs=[SMEM, HBM, VMEM, HBM, VMEM],
-        out_specs=[VMEM] * 6,
+        out_specs=[VMEM] * 4,
         scratch_shapes=[
             pltpu.VMEM((groups, slots, lanes), BF16),
-            pltpu.VMEM((ff, groups * LANES), BF16),
+            pltpu.VMEM((groups * LANES, ff), BF16),
             pltpu.SemaphoreType.DMA((3,)),
         ],
         out_shape=(
-            jax.ShapeDtypeStruct((chips, slots, lanes), BF16),
-            jax.ShapeDtypeStruct((slots, ff), BF16),
-            jax.ShapeDtypeStruct((slots, ff), BF16),
+            jax.ShapeDtypeStruct((2, slots, ff), BF16),
             jax.ShapeDtypeStruct((slots, LANES), F32),
             jax.ShapeDtypeStruct((8, slots), F32),
             jax.ShapeDtypeStruct((experts, slots), F32),
         ),
-        compiler_params=pltpu.CompilerParams(vmem_limit_bytes=47 * 1024 * 1024),
+        compiler_params=pltpu.CompilerParams(vmem_limit_bytes=EXPERT_VMEM),
         cost_estimate=pl.CostEstimate(
-            flops=4_000_000_000, bytes_accessed=16_000_000, transcendentals=slots * ff
+            flops=3_000_000_000, bytes_accessed=16_000_000, transcendentals=slots * ff
         ),
     )(at, whole, front, back, scorer)
 
-    swapped = lax.ppermute(send, "dp", swap)
+    both_other = lax.ppermute(both, "dp", swap)
     keep = call(
         keep_kernel,
         jax.ShapeDtypeStruct((chips, slots, lanes), BF16),
-        [SMEM] + [VMEM] * 5,
+        [VMEM] * 3,
         flops=2_000_000_000,
         moved=8_000_000,
-    )(at, pre, hidden, gating, front, back)
-    halves = keep + swapped
+    )(both, gating, own)
+    halves = pl.pallas_call(
+        other_kernel,
+        grid=(chips // 2,),
+        in_specs=[VMEM, VMEM, pl.BlockSpec((2, 2 * LANES, ff), lambda i: (0, i, 0)), VMEM],
+        out_specs=pl.BlockSpec((2, slots, lanes), lambda i: (i, 0, 0)),
+        out_shape=jax.ShapeDtypeStruct((chips, slots, lanes), BF16),
+        compiler_params=pltpu.CompilerParams(vmem_limit_bytes=VMEM_LIMIT),
+        cost_estimate=pl.CostEstimate(
+            flops=2_000_000_000, bytes_accessed=8_000_000, transcendentals=0
+        ),
+    )(both_other, gating, other, keep)
     halves, gate_term = lax.optimization_barrier((halves, gate_term))
     sums = lax.psum_scatter(
         halves, "dp", scatter_dimension=0, axis_index_groups=same_core, tiled=True

time: 187 us -> 188 us (level)
  waiting for transfers between devices: 55.6 us -> 50.7 us
  other arithmetic: 1.91 us -> 4.66 us
  starting transfers between devices: 21.8 us -> 23.8 us
  local copies, waits for them, and re-layouts: 12.1 us -> 14 us
    all_gather x1, waiting for transfers between devices: 28.1 us -> 22.8 us  [shards(): whole = lax.all_gather(got[None], 'dp', axis=0, tiled=True)]
    another operation x1 -> x2, other arithmetic: 0.08 us -> 4.66 us  [half(): return jnp.stack(picked).reshape(2, chips * LANES, ff)]
    pallas_call x1 -> x2, Pallas kernels: 1.88 us -> 5.96 us  [the longest x1 4.67 us: shards(): pl.pallas_call(other_kernel, grid=(chips // 2,), in_specs=[VMEM, VMEM, pl...]
    unnamed x14 -> x22, local copies, waits for them, and re-layouts: 1.11 us -> 5.05 us
    pallas_call x1, Pallas kernels: 8.16 us -> 4.88 us  [shards(): pl.pallas_call(functools.partial(expert_kernel, experts), in_specs=[SMEM,...]
    reshape x1 -> x0, local copies, waits for them, and re-layouts: 2.49 us -> none  [shards(): back = back.reshape(ff, groups * LANES)]
    dynamic_slice x0 -> x1, local copies, waits for them, and re-layouts: none -> 1.97 us  [half(): lax.dynamic_index_in_dim(part.reshape(chips, 2, LANES, ff), which, 1, kee...]
    ppermute x1 -> x2, starting transfers between devices: 2.13 us -> 4.05 us  [the longest x1 2.14 us: shards(): both_other = lax.ppermute(both, 'dp', swap)]
  transfers between devices with their start and end apart: 5 -> 6, of which waited for: 5 -> 6; matrix products, arithmetic and copies ran while one was open for 6% -> 7% of each run, Pallas kernels for 2% -> 1%
where the time goes in v5:
time: 188 us
  blocking collectives  65.6 us (35%)
  waiting for transfers between devices  50.7 us (27%)
  starting transfers between devices  23.8 us (13%)
  Pallas kernels  14.8 us (8%)
  between operations  14.2 us (8%)
  local copies, waits for them, and re-layouts  14 us (7%)
  other arithmetic  4.66 us (2%)
    all_to_all x1, blocking collectives, shards(): lax.all_to_all(mine.reshape(sources, capacity, lanes), 'expert', split_ax...  38.5 us
    all_to_all x1, blocking collectives, shards(): lax.all_to_all(home.reshape(sources, capacity, lanes), 'expert', split_ax...  27.1 us
    all_gather x1, waiting for transfers between devices, shards(): whole = lax.all_gather(got[None], 'dp', axis=0, tiled=True)  22.8 us
    all_to_all x1, starting transfers between devices, shards(): lax.all_to_all(router_part.reshape(experts, 1, LANES), 'expert', split_ax...  14 us
    all_to_all x1, waiting for transfers between devices, shards(): lax.all_to_all(router_part.reshape(experts, 1, LANES), 'expert', split_ax...  11.8 us
    reduce_scatter x1, waiting for transfers between devices, shards(): lax.psum_scatter(halves, 'dp', scatter_dimension=0, axis_index_groups=sam...  9.76 us
    all_to_all x1, starting transfers between devices, shards(): lax.all_to_all(jnp.broadcast_to(gate_term[None, :1], (groups, 1, slots)),...  5.64 us
    unnamed x22, local copies, waits for them, and re-layouts  5.05 us
  transfers between devices with their start and end apart: 6, of which 6 were waited for; matrix products, arithmetic and copies ran while one was open for 7% of the time, Pallas kernels for 1%

profile of v5, /device:TPU:6, one launch (start us, length us, event | category | flops | bytes accessed | tf_op | source)
XLA Modules:
  0.0 187.8 jit_solution(12686697039049486567)
XLA Ops:
  7.2 0.0 all-gather.3.cloned.1.call-start
  7.2 1.9 shard_map.94
  9.1 38.5 %all_to_all.20 = bf16[64,8,256]{2,1,0:T(8,128)(2,1)} all-to-all(bf16[64,8,256]{2,1,0:T(8,128)(2,1)} %bitcast.62), channel_id=1, replica_groups=mesh['expert'=64,'dp'=16] {'expert'}, dimensions={0} | all-to-all | bytes 524288 | tf_op jit(solution)/shard_map/all_to_all | solution.py:235
  47.6 0.0 all-gather.3.cloned.1.call-update
  47.6 0.0 reduce-scatter.2.cloned.1.call-start
  47.7 3.6 %copy.12 = bf16[1,512,1664]{1,2,0:T(8,128)(2,1)} copy(bf16[1,512,1664]{2,1,0:T(8,128)(2,1)} %param.12) | data formatting | bytes 3407872 | tf_op jit(solution)/shard_map/optimization_barrier | solution.py:239
  51.3 0.0 copy-start.8
  51.3 1.8 pad.16
  53.1 0.2 copy-done.8
  53.3 0.2 pad.15
  53.5 0.0 copy-start
  53.5 2.0 %constant_dynamic-slice_fusion = (bf16[8,1,128,512]{3,2,1,0:T(8,128)(2,1)}, bf16[8,1,128,512]{3,2,1,0:T(8,128)(2,1)S(1)}, bf16[8,1,128,512]{3,2,1,0:T(8,128)(2,1)S(1)}, bf16[8,1,128,512]{3,2,1,0:T(8,128)(2,1)}) fusion(bf16[8,2,128,512]{3,2,1,0:T(8,128)(2,1)S(1)} %bitcast.42, s32[]{:T(128)S(6)} %select_n.21, s32[]{:T(128)S(6)} %select_n.20, ...), kind=kLoop, calls=%fused_computation.5 | loop fusion | bytes 8388616 | tf_op jit(solution)/shard_map/jit(dynamic_index_in_dim)/dynamic_slice | solution.py:251
  55.5 0.0 copy-done
  55.5 0.0 copy-start.9
  55.5 1.5 pad_maximum_fusion
  57.0 1.9 %collective-permute-start = (bf16[2,1024,512]{2,1,0:T(8,128)(2,1)}, bf16[2,1024,512]{2,1,0:T(8,128)(2,1)}, u32[]{:S(2)}, u32[]{:S(2)}) collective-permute-start(bf16[2,1024,512]{2,1,0:T(8,128)(2,1)} %pad_maximum_fusion), channel_id=1, source_target_pairs={{0,1},{1,0},{2,3},{3,2},{4,5},{5,4},{6,7},{7,6},{8,9},{9,8},{10,11... | collective-permute-start | bytes 6291464 | tf_op jit(solution)/shard_map/ppermute | solution.py:257
  58.9 0.0 copy-done.9
  58.9 0.5 reshape.67
  59.5 0.1 pad.17
  59.6 0.1 copy.18
  59.7 3.1 %pad_maximum_fusion.1.own_ref = bf16[2,1024,512]{2,1,0:T(8,128)(2,1)} fusion(bf16[1,1024,512]{2,1,0:T(8,128)(2,1)} %bitcast.56, bf16[1,1024,512]{2,1,0:T(8,128)(2,1)} %bitcast.57), kind=kLoop, calls=%fused_computation.1 | loop fusion | flops 1048576 | bytes 4194304 | tf_op jit(solution)/shard_map/stack | solution.py:254
  62.8 0.6 collective-permute-done.own_ref
  63.4 22.8 %all-gather.3.cloned.1.call-done = bf16[8192,256]{1,0:T(8,128)(2,1)} async-done(((bf16[512,256]{1,0:T(8,128)(2,1)}), bf16[8192,256]{1,0:T(8,128)(2,1)}) %all-gather.3.cloned.1.call-update) | async-done | bytes 4194320 | tf_op jit(solution)/shard_map/all_gather | solution.py:240
  86.2 0.0 copy-start.1
  86.2 1.6 copy-done.1
  87.8 2.2 %copy-done.7 = bf16[8192,256]{1,0:T(8,128)(2,1)S(1)} copy-done((bf16[8192,256]{1,0:T(8,128)(2,1)S(1)}, bf16[8192,256]{1,0:T(8,128)(2,1)}, u32[]{:S(2)}) %copy-start.7) | copy-done | bytes 4194328
  90.0 4.9 %shard_map.95 = (bf16[2,512,512]{2,1,0:T(8,128)(2,1)S(1)}, f32[512,128]{1,0:T(8,128)S(1)}, f32[8,512]{1,0:T(8,128)S(1)}, f32[64,512]{1,0:T(8,128)S(1)}) custom-call(s32[1]{0:T(128)} %bitcast.at_ref, bf16[16,512,256]{2,1,0:T(8,128)(2,1)S(1)} %bitcast.54, bf16[2048,512]{1,0:T(8,128)(2,1)S(1)} %bitcast.45, bf16[2048,512]{1,0:T(8,128)(2,1)S(1)} %bitcast.43, ...), custom_call_target="tpu_custom_call" | custom-call | flops 3000000000 | bytes 16000000 | tf_op jit(solution)/shard_map/pallas_call | solution.py:263
  94.9 2.1 %collective-permute-start.1 = (bf16[2,512,512]{2,1,0:T(8,128)(2,1)S(1)}, bf16[2,512,512]{2,1,0:T(8,128)(2,1)S(1)}, u32[]{:S(2)}, u32[]{:S(2)}) collective-permute-start(bf16[2,512,512]{2,1,0:T(8,128)(2,1)S(1)} %get-tuple-element.29.both_ref), channel_id=1, source_target_pairs={{0,1},{1,0},{2,3},{3,2},{4,5},{5,4},{6,7},{7,6},{8,9},{9,8},{10,11... | collective-permute-start | bytes 3145736 | tf_op jit(solution)/shard_map/ppermute | solution.py:284
  97.1 0.0 copy-done.3
  97.1 1.3 shard_map.96.keep_ref
  98.4 1.1 collective-permute-done.1.both_ref
  99.5 4.7 %shard_map.97 = bf16[8,512,256]{2,1,0:T(8,128)(2,1)} custom-call(bf16[2,512,512]{2,1,0:T(8,128)(2,1)S(1)} %collective-permute-done.1.both_ref, f32[512,128]{1,0:T(8,128)S(1)} %get-tuple-element.30.gating_ref, bf16[2,1024,512]{2,1,0:T(8,128)(2,1)} %collective-permute-done.own_ref, bf16[8,512,256]{2,1,0:T(8,128)(2,1)S(1)} %shard_map.96.keep_ref), custom_call_target="tpu_custom_call" | custom-call | flops 2000000000 | bytes 8000000 | tf_op jit(solution)/shard_map/pallas_call | solution.py:292
  104.1 0.0 reduce-scatter.2.cloned.1.call-update
  104.2 0.6 broadcast_in_dim.17
  104.8 5.6 %all-to-all-start.1 = ((f32[16,1,512]{2,1,0:T(1,128)}), f32[16,1,512]{2,1,0:T(1,128)S(1)}, u32[]{:S(2)}, u32[]{:S(2)}) async-start(f32[16,1,512]{2,1,0:T(1,128)} %broadcast_in_dim.17), calls=%async_computation.2 | async-start | bytes 65536 | tf_op jit(solution)/shard_map/all_to_all | solution.py:308
  110.5 4.6 %all-to-all-done.1 = f32[16,1,512]{2,1,0:T(1,128)S(1)} async-done(((f32[16,1,512]{2,1,0:T(1,128)}), f32[16,1,512]{2,1,0:T(1,128)S(1)}, u32[]{:S(2)}, u32[]{:S(2)}) %all-to-all-start.1) | async-done | bytes 32800 | tf_op jit(solution)/shard_map/all_to_all | solution.py:308
  115.1 0.0 copy-done.2
  115.1 0.8 shard_map.98
  115.9 14.0 %all-to-all-start.2 = ((f32[64,1,128]{2,1,0:T(1,128)}), f32[64,1,128]{2,1,0:T(1,128)S(1)}, u32[]{:S(2)}, u32[]{:S(2)}) async-start(f32[64,1,128]{2,1,0:T(1,128)} %bitcast.24), calls=%async_computation.3 | async-start | bytes 65536 | tf_op jit(solution)/shard_map/all_to_all | solution.py:323
  129.9 0.1 dynamic-slice_bitcast_fusion
  130.0 11.8 %all-to-all-done.2 = f32[64,1,128]{2,1,0:T(1,128)S(1)} async-done(((f32[64,1,128]{2,1,0:T(1,128)}), f32[64,1,128]{2,1,0:T(1,128)S(1)}, u32[]{:S(2)}, u32[]{:S(2)}) %all-to-all-start.2) | async-done | bytes 32800 | tf_op jit(solution)/shard_map/all_to_all | solution.py:323
  141.8 9.8 %reduce-scatter.2.cloned.1.call-done = bf16[1,512,256]{2,1,0:T(8,128)(2,1)} async-done(((bf16[8,512,256]{2,1,0:T(8,128)(2,1)}), bf16[1,512,256]{2,1,0:T(8,128)(2,1)}) %reduce-scatter.2.cloned.1.call-update) | async-done | bytes 262160 | tf_op jit(solution)/shard_map/reduce_scatter | solution.py:304
  151.5 0.0 copy-done.6
  151.5 0.9 copy-done.4
  152.5 0.3 shard_map.99
  152.8 27.1 %all_to_all.21 = bf16[64,8,256]{2,1,0:T(8,128)(2,1)S(1)} all-to-all(bf16[64,8,256]{2,1,0:T(8,128)(2,1)S(1)} %bitcast.49), channel_id=1, replica_groups=mesh['expert'=64,'dp'=16] {'expert'}, dimensions={0} | all-to-all | bytes 524288 | tf_op jit(solution)/shard_map/all_to_all | solution.py:334
  179.9 0.0 copy-done.5
  179.9 1.0 shard_map.100
  (9 shorter events, 0.0 us)
Async XLA Ops:
  7.2 79.1 %all-gather.3.cloned.1.call-start = ((), (), s32[]{:S(2)}) async-start(), calls=%async_computation.6 | async-start | bytes 4456448 | tf_op jit(solution)/shard_map/all_gather | solution.py:240
  47.6 103.9 %reduce-scatter.2.cloned.1.call-start = ((), (), s32[]{:S(2)}) async-start(), calls=%async_computation.5 | async-start | bytes 2359296 | tf_op jit(solution)/shard_map/reduce_scatter | solution.py:304
  51.3 2.0 %copy-start.8 = (bf16[1,1664,512]{2,1,0:T(8,128)(2,1)S(1)}, bf16[1,1664,512]{2,1,0:T(8,128)(2,1)}, u32[]{:S(2)}) copy-start(bf16[1,1664,512]{2,1,0:T(8,128)(2,1)} %param.11) | copy-start | bytes 5111812
  53.5 2.0 %copy-start = (bf16[16,128,512]{2,1,0:T(8,128)(2,1)}, bf16[16,128,512]{2,1,0:T(8,128)(2,1)S(1)}, u32[]{:S(2)}) copy-start(bf16[16,128,512]{2,1,0:T(8,128)(2,1)S(1)} %pad.15) | copy-start | bytes 6291460
  55.5 3.5 %copy-start.9 = (bf16[1664,64]{0,1:T(8,128)(2,1)S(1)}, bf16[1664,64]{0,1:T(8,128)(2,1)}, u32[]{:S(2)}) copy-start(bf16[1664,64]{0,1:T(8,128)(2,1)} %param.10) | copy-start | bytes 638980
  57.0 6.4 %collective-permute-start = (bf16[2,1024,512]{2,1,0:T(8,128)(2,1)}, bf16[2,1024,512]{2,1,0:T(8,128)(2,1)}, u32[]{:S(2)}, u32[]{:S(2)}) collective-permute-start(bf16[2,1024,512]{2,1,0:T(8,128)(2,1)} %pad_maximum_fusion), channel_id=1, source_target_pairs={{0,1},{1,0},{2,3},{3,2},{4,5},{5,4},{6,7},{7,6},{8,9},{9,8},{10,11... | collective-permute-start | bytes 6291464 | tf_op jit(solution)/shard_map/ppermute | solution.py:257
  86.2 1.6 copy-start.1
  87.8 2.2 %copy-start.7 = (bf16[8192,256]{1,0:T(8,128)(2,1)S(1)}, bf16[8192,256]{1,0:T(8,128)(2,1)}, u32[]{:S(2)}) copy-start(bf16[8192,256]{1,0:T(8,128)(2,1)} %all-gather.3.cloned.1.call-done) | copy-start | bytes 12582916
  90.0 7.0 %copy-start.3 = (bf16[2,1024,512]{2,1,0:T(8,128)(2,1)S(1)}, bf16[2,1024,512]{2,1,0:T(8,128)(2,1)}, u32[]{:S(2)}) copy-start(bf16[2,1024,512]{2,1,0:T(8,128)(2,1)} %pad_maximum_fusion.1.own_ref) | copy-start | bytes 6291460
  94.9 4.6 %collective-permute-start.1 = (bf16[2,512,512]{2,1,0:T(8,128)(2,1)S(1)}, bf16[2,512,512]{2,1,0:T(8,128)(2,1)S(1)}, u32[]{:S(2)}, u32[]{:S(2)}) collective-permute-start(bf16[2,512,512]{2,1,0:T(8,128)(2,1)S(1)} %get-tuple-element.29.both_ref), channel_id=1, source_target_pairs={{0,1},{1,0},{2,3},{3,2},{4,5},{5,4},{6,7},{7,6},{8,9},{9,8},{10,11... | collective-permute-start | bytes 3145736 | tf_op jit(solution)/shard_map/ppermute | solution.py:284
  104.1 10.9 %copy-start.2 = (bf16[64,8,256]{2,1,0:T(8,128)(2,1)S(1)}, bf16[64,8,256]{2,1,0:T(8,128)(2,1)}, u32[]{:S(2)}) copy-start(bf16[64,8,256]{2,1,0:T(8,128)(2,1)} %all_to_all.20) | copy-start | bytes 786436
  104.1 47.4 %copy-start.6 = (bf16[128,128]{1,0:T(8,128)(2,1)S(1)}, bf16[128,128]{1,0:T(8,128)(2,1)}, u32[]{:S(2)}) copy-start(bf16[128,128]{1,0:T(8,128)(2,1)} %constant.44.clone.fold_ref) | copy-start | bytes 98308
  104.1 75.8 %copy-start.5 = (bf16[512,128]{1,0:T(8,128)(2,1)S(1)}, bf16[512,128]{1,0:T(8,128)(2,1)}, u32[]{:S(2)}) copy-start(bf16[512,128]{1,0:T(8,128)(2,1)} %get-tuple-element.39.pick_ref) | copy-start | bytes 393220
  104.8 10.3 %all-to-all-start.1 = ((f32[16,1,512]{2,1,0:T(1,128)}), f32[16,1,512]{2,1,0:T(1,128)S(1)}, u32[]{:S(2)}, u32[]{:S(2)}) async-start(f32[16,1,512]{2,1,0:T(1,128)} %broadcast_in_dim.17), calls=%async_computation.2 | async-start | bytes 65536 | tf_op jit(solution)/shard_map/all_to_all | solution.py:308
  115.9 25.9 %all-to-all-start.2 = ((f32[64,1,128]{2,1,0:T(1,128)}), f32[64,1,128]{2,1,0:T(1,128)S(1)}, u32[]{:S(2)}, u32[]{:S(2)}) async-start(f32[64,1,128]{2,1,0:T(1,128)} %bitcast.24), calls=%async_computation.3 | async-start | bytes 65536 | tf_op jit(solution)/shard_map/all_to_all | solution.py:323
  151.5 1.0 copy-start.4
Sparse Core Ops, SparseCore 0:
  47.7 38.4 all-gather.2
  104.3 47.1 reduce-scatter.1

commit v6 on v5

--- a/solution.py
+++ b/solution.py
@@ -11,7 +11,7 @@
 F32 = jnp.float32
 BF16 = jnp.bfloat16
 LANES = 128
-EXPERT_VMEM = 42 * 1024 * 1024
+EXPERT_VMEM = 49 * 1024 * 1024
 VMEM_LIMIT = 24 * 1024 * 1024
 VMEM = pl.BlockSpec(memory_space=pltpu.VMEM)
 HBM = pl.BlockSpec(memory_space=pltpu.HBM)
@@ -60,7 +60,7 @@
 
 
 def terms(both_ref, gating_ref, own_ref, pair):
-    rows = slice(pair * 2 * LANES, (pair + 1) * 2 * LANES)
+    rows = pl.ds(pair * 2 * LANES, 2 * LANES)
     grad = dot(both_ref[0], own_ref[0, rows, :], ((1,), (1,)))
     out = dot(both_ref[1], own_ref[1, rows, :], ((1,), (1,)))
     for j in range(2):
@@ -80,10 +80,11 @@
     gate_ref,
     chance_ref,
     got,
+    deep,
     wide,
     sems,
 ):
-    parts = sems.shape[0] - 1
+    parts = sems.shape[0] - 2
     groups, slots = got.shape[0], got.shape[1]
     chunk = slots // parts
     own = at_ref[0]
@@ -92,16 +93,19 @@
         rows = pl.ds(i * chunk, chunk)
         copies.append(pltpu.make_async_copy(whole_ref.at[:, rows], got.at[:, rows], sems.at[i]))
     wide_copy = pltpu.make_async_copy(back_ref, wide, sems.at[parts])
+    deep_copy = pltpu.make_async_copy(front_ref, deep, sems.at[parts + 1])
+    deep_copy.start()
     copies[0].start()
     wide_copy.start()
     for copy in copies[1:]:
         copy.start()
+    deep_copy.wait()
     for i in range(parts):
         copies[i].wait()
         rows = slice(i * chunk, (i + 1) * chunk)
         tok = jnp.concatenate([got[j, rows, :LANES] for j in range(groups)], axis=1)
         cot = jnp.concatenate([got[j, rows, LANES:] for j in range(groups)], axis=1)
-        x = dot(tok, front_ref[...])
+        x = dot(tok, deep[...])
         scores = dot(tok, router_ref[...], ((1,), (1,)))
         if i == 0:
             wide_copy.wait()
@@ -127,19 +131,28 @@
         gate_ref[:, rows] = turned[experts : experts + 8]
 
 
-def keep_kernel(both_ref, gating_ref, own_ref, keep_ref):
+def keep_kernel(both_ref, gating_ref, own_ref, other_ref, keep_ref, near_ref, sem):
+    copy = pltpu.make_async_copy(other_ref, near_ref, sem)
+    copy.start()
     for pair in range(keep_ref.shape[0] // 2):
         for j, grad, out in terms(both_ref, gating_ref, own_ref, pair):
             keep_ref[2 * pair + j, :, :LANES] = grad.astype(BF16)
             keep_ref[2 * pair + j, :, LANES:] = out.astype(BF16)
-
-
-def other_kernel(both_ref, gating_ref, own_ref, keep_ref, sum_ref):
-    pair = pl.program_id(0)
-    for j, grad, out in terms(both_ref, gating_ref, own_ref, 0):
-        kept = keep_ref[2 * pair + j].astype(F32)
-        sum_ref[j, :, :LANES] = (grad + kept[:, :LANES]).astype(BF16)
-        sum_ref[j, :, LANES:] = (out + kept[:, LANES:]).astype(BF16)
+    copy.wait()
+
+
+def other_kernel(both_ref, gating_ref, own_ref, keep_ref, sum_ref, stage, sems):
+    copies = []
+    for pair in range(keep_ref.shape[0] // 2):
+        for j, grad, out in terms(both_ref, gating_ref, own_ref, pair):
+            kept = keep_ref[2 * pair + j].astype(F32)
+            stage[2 * pair + j, :, :LANES] = (grad + kept[:, :LANES]).astype(BF16)
+            stage[2 * pair + j, :, LANES:] = (out + kept[:, LANES:]).astype(BF16)
+        two = pl.ds(2 * pair, 2)
+        copies.append(pltpu.make_async_copy(stage.at[two], sum_ref.at[two], sems.at[pair]))
+        copies[pair].start()
+    for copy in copies:
+        copy.wait()
 
 
 def router_kernel(at_ref, gates_ref, chance_ref, slots_ref, score_ref, part_ref):
@@ -262,12 +275,13 @@
     whole, other, own = lax.optimization_barrier((whole, other, own))
     both, gating, gate_term, chances = pl.pallas_call(
         functools.partial(expert_kernel, experts),
-        in_specs=[SMEM, HBM, VMEM, HBM, VMEM],
+        in_specs=[SMEM, HBM, HBM, HBM, VMEM],
         out_specs=[VMEM] * 4,
         scratch_shapes=[
             pltpu.VMEM((groups, slots, lanes), BF16),
             pltpu.VMEM((groups * LANES, ff), BF16),
-            pltpu.SemaphoreType.DMA((3,)),
+            pltpu.VMEM((groups * LANES, ff), BF16),
+            pltpu.SemaphoreType.DMA((4,)),
         ],
         out_shape=(
             jax.ShapeDtypeStruct((2, slots, ff), BF16),
@@ -282,24 +296,34 @@
     )(at, whole, front, back, scorer)
 
     both_other = lax.ppermute(both, "dp", swap)
-    keep = call(
-        keep_kernel,
-        jax.ShapeDtypeStruct((chips, slots, lanes), BF16),
-        [VMEM] * 3,
-        flops=2_000_000_000,
-        moved=8_000_000,
-    )(both, gating, own)
-    halves = pl.pallas_call(
-        other_kernel,
-        grid=(chips // 2,),
-        in_specs=[VMEM, VMEM, pl.BlockSpec((2, 2 * LANES, ff), lambda i: (0, i, 0)), VMEM],
-        out_specs=pl.BlockSpec((2, slots, lanes), lambda i: (i, 0, 0)),
-        out_shape=jax.ShapeDtypeStruct((chips, slots, lanes), BF16),
+    terms_params = dict(
         compiler_params=pltpu.CompilerParams(vmem_limit_bytes=VMEM_LIMIT),
         cost_estimate=pl.CostEstimate(
             flops=2_000_000_000, bytes_accessed=8_000_000, transcendentals=0
         ),
-    )(both_other, gating, other, keep)
+    )
+    keep, near = pl.pallas_call(
+        keep_kernel,
+        in_specs=[VMEM, VMEM, VMEM, HBM],
+        out_specs=[VMEM] * 2,
+        out_shape=(
+            jax.ShapeDtypeStruct((chips, slots, lanes), BF16),
+            jax.ShapeDtypeStruct(other.shape, BF16),
+        ),
+        scratch_shapes=[pltpu.SemaphoreType.DMA],
+        **terms_params,
+    )(both, gating, own, other)
+    halves = pl.pallas_call(
+        other_kernel,
+        in_specs=[VMEM] * 4,
+        out_specs=HBM,
+        out_shape=jax.ShapeDtypeStruct((chips, slots, lanes), BF16),
+        scratch_shapes=[
+            pltpu.VMEM((chips, slots, lanes), BF16),
+            pltpu.SemaphoreType.DMA((chips // 2,)),
+        ],
+        **terms_params,
+    )(both_other, gating, near, keep)
     halves, gate_term = lax.optimization_barrier((halves, gate_term))
     sums = lax.psum_scatter(
         halves, "dp", scatter_dimension=0, axis_index_groups=same_core, tiled=True

time: 188 us -> 184 us (0.979)
  local copies, waits for them, and re-layouts: 14 us -> 9.31 us
    pallas_call x2, Pallas kernels: 5.96 us -> 3.74 us  [the longest x1 2.14 us: shards(): pl.pallas_call(other_kernel, in_specs=[VMEM] * 4, out_specs=HBM, out_shap...]
    unnamed x22 -> x18, local copies, waits for them, and re-layouts: 5.05 us -> 2.97 us
  transfers between devices with their start and end apart: 6 -> 6, of which waited for: 6 -> 6; matrix products, arithmetic and copies ran while one was open for 7% -> 6% of each run, Pallas kernels for 1% -> 1%
where the time goes in v6:
time: 184 us; the launch traced here: 183 us
  blocking collectives  66 us (36%)
  waiting for transfers between devices  51.1 us (28%)
  starting transfers between devices  23.7 us (13%)
  between operations  14.2 us (8%)
  Pallas kernels  14 us (8%)
  local copies, waits for them, and re-layouts  9.31 us (5%)
  other arithmetic  4.65 us (3%)
    all_to_all x1, blocking collectives, shards(): lax.all_to_all(mine.reshape(sources, capacity, lanes), 'expert', split_ax...  38.5 us
    all_to_all x1, blocking collectives, shards(): lax.all_to_all(home.reshape(sources, capacity, lanes), 'expert', split_ax...  27.5 us
    all_gather x1, waiting for transfers between devices, shards(): whole = lax.all_gather(got[None], 'dp', axis=0, tiled=True)  23.8 us
    all_to_all x1, starting transfers between devices, shards(): lax.all_to_all(router_part.reshape(experts, 1, LANES), 'expert', split_ax...  14 us
    all_to_all x1, waiting for transfers between devices, shards(): lax.all_to_all(router_part.reshape(experts, 1, LANES), 'expert', split_ax...  11.8 us
    reduce_scatter x1, waiting for transfers between devices, shards(): lax.psum_scatter(halves, 'dp', scatter_dimension=0, axis_index_groups=sam...  9.52 us
    pallas_call x1, Pallas kernels, shards(): pl.pallas_call(functools.partial(expert_kernel, experts), in_specs=[SMEM,...  6.32 us
    all_to_all x1, starting transfers between devices, shards(): lax.all_to_all(jnp.broadcast_to(gate_term[None, :1], (groups, 1, slots)),...  5.65 us
  transfers between devices with their start and end apart: 6, of which 6 were waited for; matrix products, arithmetic and copies ran while one was open for 6% of the time, Pallas kernels for 1%

profile of v6, /device:TPU:6, one launch (start us, length us, event | category | flops | bytes accessed | tf_op | source)
XLA Modules:
  0.0 183.0 jit_solution(12285953210844239998)
XLA Ops:
  7.2 0.0 all-gather.3.cloned.1.call-start
  7.2 1.8 %shard_map.94 = (bf16[512,256]{1,0:T(8,128)(2,1)}, bf16[512,128]{1,0:T(8,128)(2,1)}) custom-call(s32[2,128]{1,0:T(2,128)} %bitcast.70, bf16[104,128]{1,0:T(8,128)(2,1)} %bitcast.66, bf16[104,128]{1,0:T(8,128)(2,1)} %bitcast.67), custom_call_target="tpu_custom_call" | custom-call | flops 60000000 | bytes 500000 | tf_op jit(solution)/shard_map/pallas_call | solution.py:227
  9.0 38.5 %all_to_all.20 = bf16[64,8,256]{2,1,0:T(8,128)(2,1)} all-to-all(bf16[64,8,256]{2,1,0:T(8,128)(2,1)} %bitcast.61), channel_id=1, replica_groups=mesh['expert'=64,'dp'=16] {'expert'}, dimensions={0} | all-to-all | bytes 524288 | tf_op jit(solution)/shard_map/all_to_all | solution.py:248
  47.5 0.0 all-gather.3.cloned.1.call-update
  47.6 0.0 reduce-scatter.2.cloned.1.call-start
  47.6 2.8 %copy.12 = bf16[1,512,1664]{1,2,0:T(8,128)(2,1)S(1)} copy(bf16[1,512,1664]{2,1,0:T(8,128)(2,1)} %param.12) | data formatting | bytes 3407872 | tf_op jit(solution)/shard_map/optimization_barrier | solution.py:252
  50.5 0.0 copy-start.6
  50.5 0.2 pad.16
  50.7 0.0 copy-start.5
  50.7 1.8 %copy-done.6 = bf16[1,1664,512]{2,1,0:T(8,128)(2,1)S(1)} copy-done((bf16[1,1664,512]{2,1,0:T(8,128)(2,1)S(1)}, bf16[1,1664,512]{2,1,0:T(8,128)(2,1)}, u32[]{:S(2)}) %copy-start.6) | copy-done | bytes 1703960
  52.6 0.2 pad.15
  52.8 1.7 constant_dynamic-slice_fusion
  54.5 0.0 copy-done.5
  54.5 0.0 copy-start.7
  54.5 1.5 pad_maximum_fusion
  56.1 1.9 %collective-permute-start = (bf16[2,1024,512]{2,1,0:T(8,128)(2,1)}, bf16[2,1024,512]{2,1,0:T(8,128)(2,1)}, u32[]{:S(2)}, u32[]{:S(2)}) collective-permute-start(bf16[2,1024,512]{2,1,0:T(8,128)(2,1)} %pad_maximum_fusion), channel_id=1, source_target_pairs={{0,1},{1,0},{2,3},{3,2},{4,5},{5,4},{6,7},{7,6},{8,9},{9,8},{10,11... | collective-permute-start | bytes 6291464 | tf_op jit(solution)/shard_map/ppermute | solution.py:270
  58.0 0.0 copy-done.7
  58.0 0.5 reshape.67
  58.5 0.1 pad.17
  58.6 0.1 copy.18
  58.8 3.1 %pad_maximum_fusion.1.own_ref = bf16[2,1024,512]{2,1,0:T(8,128)(2,1)} fusion(bf16[1,1024,512]{2,1,0:T(8,128)(2,1)} %bitcast.55, bf16[1,1024,512]{2,1,0:T(8,128)(2,1)} %bitcast.56), kind=kLoop, calls=%fused_computation.1 | loop fusion | flops 1048576 | bytes 4194304 | tf_op jit(solution)/shard_map/stack | solution.py:267
  61.9 0.6 collective-permute-done.other_ref
  62.4 23.8 %all-gather.3.cloned.1.call-done = bf16[8192,256]{1,0:T(8,128)(2,1)} async-done(((bf16[512,256]{1,0:T(8,128)(2,1)}), bf16[8192,256]{1,0:T(8,128)(2,1)}) %all-gather.3.cloned.1.call-update) | async-done | bytes 4194320 | tf_op jit(solution)/shard_map/all_gather | solution.py:253
  86.2 6.3 %shard_map.95 = (bf16[2,512,512]{2,1,0:T(8,128)(2,1)S(1)}, f32[512,128]{1,0:T(8,128)S(1)}, f32[8,512]{1,0:T(8,128)S(1)}, f32[64,512]{1,0:T(8,128)S(1)}) custom-call(s32[1]{0:T(128)} %bitcast.at_ref, bf16[16,512,256]{2,1,0:T(8,128)(2,1)} %bitcast.64, bf16[2048,512]{1,0:T(8,128)(2,1)S(1)} %bitcast.43, bf16[2048,512]{1,0:T(8,128)(2,1)} %bitcast.53, ...), custom_call_target="tpu_custom_call" | custom-call | flops 3000000000 | bytes 16000000 | tf_op jit(solution)/shard_map/pallas_call | solution.py:276
  92.6 2.1 %collective-permute-start.1 = (bf16[2,512,512]{2,1,0:T(8,128)(2,1)S(1)}, bf16[2,512,512]{2,1,0:T(8,128)(2,1)S(1)}, u32[]{:S(2)}, u32[]{:S(2)}) collective-permute-start(bf16[2,512,512]{2,1,0:T(8,128)(2,1)S(1)} %get-tuple-element.31.both_ref), channel_id=1, source_target_pairs={{0,1},{1,0},{2,3},{3,2},{4,5},{5,4},{6,7},{7,6},{8,9},{9,8},{10,11... | collective-permute-start | bytes 3145736 | tf_op jit(solution)/shard_map/ppermute | solution.py:298
  94.7 0.0 copy-done.1
  94.7 1.6 shard_map.96
  96.3 0.8 collective-permute-done.1.both_ref
  97.1 2.1 %shard_map.97 = bf16[8,512,256]{2,1,0:T(8,128)(2,1)} custom-call(bf16[2,512,512]{2,1,0:T(8,128)(2,1)S(1)} %collective-permute-done.1.both_ref, f32[512,128]{1,0:T(8,128)S(1)} %get-tuple-element.32.gating_ref, bf16[2,1024,512]{2,1,0:T(8,128)(2,1)S(1)} %get-tuple-element.35.own_ref, bf16[8,512,256]{2,1,0:T(8,128)(2,1)S(1)} %get-tuple-element.36.keep_ref), custom_call_target="tpu_custom_call" | custom-call | flops 2000000000 | bytes 8000000 | tf_op jit(solution)/shard_map/pallas_call | solution.py:316
  99.3 0.0 copy-start
  99.3 0.0 copy-start.4
  99.3 0.0 copy-start.3
  99.3 0.0 reduce-scatter.2.cloned.1.call-update
  99.3 0.6 broadcast_in_dim.17
  100.0 5.7 %all-to-all-start.1 = ((f32[16,1,512]{2,1,0:T(1,128)}), f32[16,1,512]{2,1,0:T(1,128)S(1)}, u32[]{:S(2)}, u32[]{:S(2)}) async-start(f32[16,1,512]{2,1,0:T(1,128)} %broadcast_in_dim.17), calls=%async_computation.2 | async-start | bytes 65536 | tf_op jit(solution)/shard_map/all_to_all | solution.py:332
  105.6 4.6 %all-to-all-done.1 = f32[16,1,512]{2,1,0:T(1,128)S(1)} async-done(((f32[16,1,512]{2,1,0:T(1,128)}), f32[16,1,512]{2,1,0:T(1,128)S(1)}, u32[]{:S(2)}, u32[]{:S(2)}) %all-to-all-start.1) | async-done | bytes 32800 | tf_op jit(solution)/shard_map/all_to_all | solution.py:332
  110.2 0.0 copy-done
  110.2 0.8 shard_map.98
  111.0 14.0 %all-to-all-start.2 = ((f32[64,1,128]{2,1,0:T(1,128)}), f32[64,1,128]{2,1,0:T(1,128)S(1)}, u32[]{:S(2)}, u32[]{:S(2)}) async-start(f32[64,1,128]{2,1,0:T(1,128)} %bitcast.24), calls=%async_computation.3 | async-start | bytes 65536 | tf_op jit(solution)/shard_map/all_to_all | solution.py:347
  125.0 0.1 dynamic-slice_bitcast_fusion
  125.1 11.8 %all-to-all-done.2 = f32[64,1,128]{2,1,0:T(1,128)S(1)} async-done(((f32[64,1,128]{2,1,0:T(1,128)}), f32[64,1,128]{2,1,0:T(1,128)S(1)}, u32[]{:S(2)}, u32[]{:S(2)}) %all-to-all-start.2) | async-done | bytes 32800 | tf_op jit(solution)/shard_map/all_to_all | solution.py:347
  136.9 9.5 %reduce-scatter.2.cloned.1.call-done = bf16[1,512,256]{2,1,0:T(8,128)(2,1)} async-done(((bf16[8,512,256]{2,1,0:T(8,128)(2,1)}), bf16[1,512,256]{2,1,0:T(8,128)(2,1)}) %reduce-scatter.2.cloned.1.call-update) | async-done | bytes 262160 | tf_op jit(solution)/shard_map/reduce_scatter | solution.py:328
  146.4 0.0 copy-done.4
  146.4 0.9 copy-done.2
  147.4 0.3 shard_map.99
  147.7 27.5 %all_to_all.21 = bf16[64,8,256]{2,1,0:T(8,128)(2,1)S(1)} all-to-all(bf16[64,8,256]{2,1,0:T(8,128)(2,1)S(1)} %bitcast.47), channel_id=1, replica_groups=mesh['expert'=64,'dp'=16] {'expert'}, dimensions={0} | all-to-all | bytes 524288 | tf_op jit(solution)/shard_map/all_to_all | solution.py:358
  175.2 0.0 copy-done.3
  175.2 1.0 shard_map.100
  (5 shorter events, 0.0 us)
Async XLA Ops:
  7.2 79.1 %all-gather.3.cloned.1.call-start = ((), (), s32[]{:S(2)}) async-start(), calls=%async_computation.6 | async-start | bytes 4456448 | tf_op jit(solution)/shard_map/all_gather | solution.py:253
  47.6 98.8 %reduce-scatter.2.cloned.1.call-start = ((), (), s32[]{:S(2)}) async-start(), calls=%async_computation.5 | async-start | bytes 2359296 | tf_op jit(solution)/shard_map/reduce_scatter | solution.py:328
  50.5 2.1 %copy-start.6 = (bf16[1,1664,512]{2,1,0:T(8,128)(2,1)S(1)}, bf16[1,1664,512]{2,1,0:T(8,128)(2,1)}, u32[]{:S(2)}) copy-start(bf16[1,1664,512]{2,1,0:T(8,128)(2,1)} %param.11) | copy-start | bytes 5111812
  50.7 3.8 %copy-start.5 = (bf16[16,128,512]{2,1,0:T(8,128)(2,1)}, bf16[16,128,512]{2,1,0:T(8,128)(2,1)S(1)}, u32[]{:S(2)}) copy-start(bf16[16,128,512]{2,1,0:T(8,128)(2,1)S(1)} %pad.16) | copy-start | bytes 6291460
  54.5 3.4 %copy-start.7 = (bf16[1664,64]{0,1:T(8,128)(2,1)S(1)}, bf16[1664,64]{0,1:T(8,128)(2,1)}, u32[]{:S(2)}) copy-start(bf16[1664,64]{0,1:T(8,128)(2,1)} %param.10) | copy-start | bytes 638980
  56.1 6.4 %collective-permute-start = (bf16[2,1024,512]{2,1,0:T(8,128)(2,1)}, bf16[2,1024,512]{2,1,0:T(8,128)(2,1)}, u32[]{:S(2)}, u32[]{:S(2)}) collective-permute-start(bf16[2,1024,512]{2,1,0:T(8,128)(2,1)} %pad_maximum_fusion), channel_id=1, source_target_pairs={{0,1},{1,0},{2,3},{3,2},{4,5},{5,4},{6,7},{7,6},{8,9},{9,8},{10,11... | collective-permute-start | bytes 6291464 | tf_op jit(solution)/shard_map/ppermute | solution.py:270
  86.2 8.5 %copy-start.1 = (bf16[2,1024,512]{2,1,0:T(8,128)(2,1)S(1)}, bf16[2,1024,512]{2,1,0:T(8,128)(2,1)}, u32[]{:S(2)}) copy-start(bf16[2,1024,512]{2,1,0:T(8,128)(2,1)} %pad_maximum_fusion.1.own_ref) | copy-start | bytes 6291460
  92.6 4.6 %collective-permute-start.1 = (bf16[2,512,512]{2,1,0:T(8,128)(2,1)S(1)}, bf16[2,512,512]{2,1,0:T(8,128)(2,1)S(1)}, u32[]{:S(2)}, u32[]{:S(2)}) collective-permute-start(bf16[2,512,512]{2,1,0:T(8,128)(2,1)S(1)} %get-tuple-element.31.both_ref), channel_id=1, source_target_pairs={{0,1},{1,0},{2,3},{3,2},{4,5},{5,4},{6,7},{7,6},{8,9},{9,8},{10,11... | collective-permute-start | bytes 3145736 | tf_op jit(solution)/shard_map/ppermute | solution.py:298
  99.3 11.0 %copy-start = (bf16[64,8,256]{2,1,0:T(8,128)(2,1)S(1)}, bf16[64,8,256]{2,1,0:T(8,128)(2,1)}, u32[]{:S(2)}) copy-start(bf16[64,8,256]{2,1,0:T(8,128)(2,1)} %all_to_all.20) | copy-start | bytes 786436
  99.3 47.1 %copy-start.4 = (bf16[128,128]{1,0:T(8,128)(2,1)S(1)}, bf16[128,128]{1,0:T(8,128)(2,1)}, u32[]{:S(2)}) copy-start(bf16[128,128]{1,0:T(8,128)(2,1)} %constant.44.clone.fold_ref) | copy-start | bytes 98308
  99.3 75.9 %copy-start.3 = (bf16[512,128]{1,0:T(8,128)(2,1)S(1)}, bf16[512,128]{1,0:T(8,128)(2,1)}, u32[]{:S(2)}) copy-start(bf16[512,128]{1,0:T(8,128)(2,1)} %get-tuple-element.43.pick_ref) | copy-start | bytes 393220
  100.0 10.3 %all-to-all-start.1 = ((f32[16,1,512]{2,1,0:T(1,128)}), f32[16,1,512]{2,1,0:T(1,128)S(1)}, u32[]{:S(2)}, u32[]{:S(2)}) async-start(f32[16,1,512]{2,1,0:T(1,128)} %broadcast_in_dim.17), calls=%async_computation.2 | async-start | bytes 65536 | tf_op jit(solution)/shard_map/all_to_all | solution.py:332
  111.0 25.9 %all-to-all-start.2 = ((f32[64,1,128]{2,1,0:T(1,128)}), f32[64,1,128]{2,1,0:T(1,128)S(1)}, u32[]{:S(2)}, u32[]{:S(2)}) async-start(f32[64,1,128]{2,1,0:T(1,128)} %bitcast.24), calls=%async_computation.3 | async-start | bytes 65536 | tf_op jit(solution)/shard_map/all_to_all | solution.py:347
  146.4 1.0 copy-start.2
Sparse Core Ops, SparseCore 0:
  47.7 38.4 all-gather.2
  99.4 46.9 reduce-scatter.1
